TPU v7x, 32 devices: a whole 2x2x4 slice. The times are simulated.
32 devices in a mesh: dp: 32 (over z, y, x, core).
Axes of the slice: x: 2, y: 2, z: 4, core: 2. Of those that a mesh axis runs over, the one named last changes fastest.
Arguments:
- inputs: bfloat16 [128, 199, 512], P('dp'), may hold values from -6 to 6
- weights: bfloat16 [2, 262144], replicated, may hold values from -0.1875 to 0.1875
- ln_gain: float32 [512], replicated, may hold values from 0.45 to 2.16
- ln_bias: float32 [512], replicated, may hold values from -3 to 3
- projection: bfloat16 [512, 1024], replicated, may hold values from -0.25 to 0.25
- targets: float32 [128, 1024], P('dp'), may hold values from -6 to 6
- master: float32 [2, 262144], P(None, 'dp'), may hold values from -0.006 to 0.006
- first_moment: float32 [2, 262144], P(None, 'dp'), may hold values from -0.0006 to 0.0006
- second_moment: float32 [2, 262144], P(None, 'dp'), may hold values from 1e-11 to 1e-08
Outputs:
- input_grad: bfloat16 [128, 199, 512], P('dp')
- update: float32 [2, 262144], P(None, 'dp')
- new_master: float32 [2, 262144], P(None, 'dp')
- new_first: float32 [2, 262144], P(None, 'dp')
- new_second: float32 [2, 262144], P(None, 'dp')
- new_weights: bfloat16 [2, 262144], replicated
All inputs are finite; a program needn't handle non-finite values.
Results may differ from a plain program's by a relative error of at most 0.006.
Values may be sent and summed in bfloat16 or wider, within the bound.
A program may use at most 64 MiB of HBM per device.

v0:
```python
import jax
import jax.numpy as jnp
from jax import lax
from jax.sharding import PartitionSpec as P


def norm_act(pre, gain, bias):
    center = pre - jnp.mean(pre, axis=-1, keepdims=True)
    spread = jnp.mean(center * center, axis=-1, keepdims=True)
    normed = center * lax.rsqrt(spread + 1e-05)
    return jax.nn.gelu(normed * gain + bias, approximate=False)


def local_pass(inputs, weights, ln_gain, ln_bias, projection, targets):
    clips, frames_in, chans = inputs.shape
    taps = weights.shape[0]
    frames_out = (frames_in - taps) // taps + 1
    windows = inputs[:, : frames_out * taps].reshape(clips, frames_out, taps, chans)
    kernel = weights.reshape(taps, chans, chans)
    pre = jnp.einsum("bfki,koi->bfo", windows, kernel, preferred_element_type=jnp.float32)
    act, pull = jax.vjp(lambda value: norm_act(value, ln_gain, ln_bias), pre)
    pooled = jnp.mean(act, axis=1).astype(jnp.bfloat16)
    predicted = jnp.dot(pooled, projection, preferred_element_type=jnp.float32)
    miss = (predicted - targets).astype(jnp.bfloat16)
    back = lax.dot_general(
        miss, projection, (((1,), (1,)), ((), ())), preferred_element_type=jnp.float32
    )
    upstream = jnp.broadcast_to(back[:, None, :] / frames_out, act.shape)
    dpre = pull(upstream)[0].astype(jnp.bfloat16)
    dwin = jnp.einsum("bfo,koi->bfki", dpre, kernel, preferred_element_type=jnp.float32).astype(
        jnp.bfloat16
    )
    dinput = dwin.reshape(clips, frames_out * taps, chans)
    tail = jnp.zeros((clips, frames_in - frames_out * taps, chans), jnp.bfloat16)
    return (windows, dpre, jnp.concatenate([dinput, tail], axis=1))


def body(
    inputs, weights, ln_gain, ln_bias, projection, targets, master, first_moment, second_moment
):
    windows, dpre, input_grad = local_pass(inputs, weights, ln_gain, ln_bias, projection, targets)
    taps = weights.shape[0]
    term = jnp.einsum("bfo,bfki->koi", dpre, windows, preferred_element_type=jnp.float32)
    summed = lax.psum(term.reshape(taps, -1), "dp")
    squares = jnp.sum(summed * summed)
    width = master.shape[1]
    grad = lax.dynamic_slice_in_dim(summed, lax.axis_index("dp") * width, width, 1)
    scale = jnp.minimum(1.0, 1.0 / (jnp.sqrt(squares) + 1e-06))
    clipped = scale * grad
    new_first = 0.9 * first_moment + 0.1 * clipped
    new_second = 0.999 * second_moment + 0.001 * clipped * clipped
    update = new_first / (1.0 - 0.9**20) / (jnp.sqrt(new_second / (1.0 - 0.999**20)) + 1e-08)
    new_master = master - 0.0001 * (update + 0.01 * master)
    new_weights = lax.all_gather(new_master.astype(jnp.bfloat16), "dp", axis=1, tiled=True)
    return (input_grad, update, new_master, new_first, new_second, new_weights)


def solution(mesh):
    return jax.shard_map(
        body,
        mesh=mesh,
        in_specs=(
            P("dp", None, None),
            P(),
            P(),
            P(),
            P(),
            P("dp", None),
            P(None, "dp"),
            P(None, "dp"),
            P(None, "dp"),
        ),
        out_specs=(
            P("dp", None, None),
            P(None, "dp"),
            P(None, "dp"),
            P(None, "dp"),
            P(None, "dp"),
            P(),
        ),
        check_vma=False,
    )
```

profile of v0, /device:TPU:0, one launch (start us, length us, event | category | flops | bytes accessed | tf_op | source)
XLA Modules:
  0.0 225.9 jit_solution(15078498607170057342)
XLA Ops:
  7.2 0.0 copy-start
  7.2 0.0 all-reduce.3.cloned.1.call-start
  7.2 1.5 slice.3
  8.7 0.0 copy-start.1
  8.7 0.0 copy-start.8
  8.8 0.0 copy-start.9
  8.8 2.3 %fusion.26 = (f32[4,99]{1,0:T(4,128)S(1)}, f32[4,99,512]{2,1,0:T(8,128)S(1)}) fusion(bf16[1,2,512,512]{3,1,2,0:T(2,128)(2,1)} %bitcast.35, bf16[4,99,2,512]{3,0,2,1:T(4,128)(2,1)S(1)} %bitcast.32), kind=kOutput, calls=%fused_computation.55 | convolution fusion | flops 415438464 | bytes 2672176 | tf_op jit(solution)/shard_map/bfki,koi->bfo/dot_general | solution.py:20
  11.1 0.0 copy-start.10
  11.1 0.3 multiply_reduce_fusion.3
  11.3 0.0 copy-done.1
  11.4 0.0 copy-done.8
  11.4 0.0 copy-done.9
  11.4 2.2 multiply_reduce_fusion.2
  13.6 0.0 copy-done
  13.6 0.0 copy-done.10
  13.6 0.5 broadcast_multiply_fusion
  14.1 0.0 copy-start.2
  14.1 0.7 multiply_reduce_fusion.1
  14.9 0.8 fusion.24
  15.7 0.0 copy-start.3
  15.8 0.9 copy-done.3
  16.6 0.0 copy-done.2
  16.6 0.9 convolution_bitcast_fusion
  17.5 2.9 %copy.23 = f32[1,2,512,512]{3,1,2,0:T(2,128)} copy(f32[1,2,512,512]{3,2,1,0:T(8,128)S(1)} %convolution_bitcast_fusion) | data formatting | bytes 4194304
  20.5 0.0 copy-start.5
  20.5 0.0 copy-start.6
  20.5 0.0 copy-start.7
  20.5 0.0 copy-start.4
  20.5 0.0 copy-start.11
  20.5 0.0 all-reduce.3.cloned.1.call-update
  20.5 0.0 all-gather.2.cloned.1.call-start
  20.6 136.6 %all-reduce.3.cloned.1.call-done = f32[2,262144]{1,0:T(2,128)} async-done(((f32[2,262144]{1,0:T(2,128)}), f32[2,262144]{1,0:T(2,128)}) %all-reduce.3.cloned.1.call-update) | async-done | bytes 2097168 | tf_op jit(solution)/shard_map/psum | solution.py:44
  157.2 4.0 %multiply_reduce_fusion = f32[]{:T(128)} fusion(f32[2,262144]{1,0:T(2,128)} %all-reduce.3.cloned.1.call-done), kind=kLoop, calls=%fused_computation | loop fusion | flops 1048575 | bytes 2097156 | tf_op jit(solution)/shard_map/reduce_sum | solution.py:45
  161.9 0.0 copy-done.5
  161.9 0.0 copy-done.6
  161.9 0.0 copy-done.7
  161.9 1.8 fusion.22
  163.7 0.0 all-gather.2.cloned.1.call-update
  163.7 0.0 copy-done.4
  163.8 0.0 copy-done.11
  163.8 0.7 convolution_convert_fusion
  164.4 0.6 copy.17
  165.1 1.2 concatenate.3
  166.3 50.2 %all-gather.2.cloned.1.call-done = bf16[2,262144]{1,0:T(2,128)(2,1)} async-done(((bf16[2,8192]{1,0:T(2,128)(2,1)}), bf16[2,262144]{1,0:T(2,128)(2,1)}) %all-gather.2.cloned.1.call-update) | async-done | bytes 1048592 | tf_op jit(solution)/shard_map/all_gather | solution.py:54
  216.5 2.6 %copy.42 = bf16[2,262144]{1,0:T(2,128)(2,1)} copy(bf16[2,262144]{1,0:T(2,128)(2,1)} %all-gather.2.cloned.1.call-done) | data formatting | bytes 2097152
  (4 shorter events, 0.0 us)
Async XLA Ops:
  7.2 6.5 %copy-start = (bf16[512,1024]{1,0:T(8,128)(2,1)S(1)}, bf16[512,1024]{1,0:T(8,128)(2,1)}, u32[]{:S(2)}) copy-start(bf16[512,1024]{1,0:T(8,128)(2,1)} %param.13) | copy-start | bytes 3145732
  7.2 150.0 %all-reduce.3.cloned.1.call-start = ((), (), s32[]{:S(2)}) async-start(), calls=%async_computation | async-start | bytes 4194304 | tf_op jit(solution)/shard_map/psum | solution.py:44
  8.7 2.6 %copy-start.1 = (bf16[4,198,512]{2,0,1:T(4,128)(2,1)}, bf16[4,198,512]{2,0,1:T(4,128)(2,1)S(1)}, u32[]{:S(2)}) copy-start(bf16[4,198,512]{2,0,1:T(4,128)(2,1)S(1)} %slice.3) | copy-start | bytes 2433028
  8.7 2.6 %copy-start.8 = (f32[512]{0:T(512)S(1)}, f32[512]{0:T(512)}, u32[]{:S(2)}) copy-start(f32[512]{0:T(512)} %param.12) | copy-start | bytes 6148
  8.8 2.6 %copy-start.9 = (f32[512]{0:T(512)S(1)}, f32[512]{0:T(512)}, u32[]{:S(2)}) copy-start(f32[512]{0:T(512)} %param.11) | copy-start | bytes 6148
  11.1 2.6 %copy-start.10 = (f32[4,1024]{1,0:T(4,128)S(1)}, f32[4,1024]{1,0:T(4,128)}, u32[]{:S(2)}) copy-start(f32[4,1024]{1,0:T(4,128)} %param.14) | copy-start | bytes 49156
  14.1 2.5 %copy-start.2 = (bf16[4,198,512]{2,0,1:T(4,128)(2,1)S(1)}, bf16[4,198,512]{2,0,1:T(4,128)(2,1)}, u32[]{:S(2)}) copy-start(bf16[4,198,512]{2,0,1:T(4,128)(2,1)} %copy-done.1) | copy-start | bytes 2433028
  15.7 0.9 copy-start.3
  20.5 141.4 %copy-start.5 = (f32[2,8192]{1,0:T(2,128)S(1)}, f32[2,8192]{1,0:T(2,128)}, u32[]{:S(2)}) copy-start(f32[2,8192]{1,0:T(2,128)} %param.15) | copy-start | bytes 196612
  20.5 141.4 %copy-start.6 = (f32[2,8192]{1,0:T(2,128)S(1)}, f32[2,8192]{1,0:T(2,128)}, u32[]{:S(2)}) copy-start(f32[2,8192]{1,0:T(2,128)} %param.16) | copy-start | bytes 196612
  20.5 141.4 %copy-start.7 = (f32[2,8192]{1,0:T(2,128)S(1)}, f32[2,8192]{1,0:T(2,128)}, u32[]{:S(2)}) copy-start(f32[2,8192]{1,0:T(2,128)} %param.17) | copy-start | bytes 196612
  20.5 143.3 %copy-start.4 = (f32[4,99,512]{2,1,0:T(8,128)S(1)}, f32[4,99,512]{2,1,0:T(8,128)}, u32[]{:S(2)}) copy-start(f32[4,99,512]{2,1,0:T(8,128)} %copy-done.3) | copy-start | bytes 2433028
  20.5 143.3 %copy-start.11 = (bf16[2,262144]{1,0:T(2,128)(2,1)S(1)}, bf16[2,262144]{1,0:T(2,128)(2,1)}, u32[]{:S(2)}) copy-start(bf16[2,262144]{1,0:T(2,128)(2,1)} %param.10) | copy-start | bytes 3145732
  20.5 195.9 %all-gather.2.cloned.1.call-start = ((), (), s32[]{:S(2)}) async-start(), calls=%async_computation.1 | async-start | bytes 1081344 | tf_op jit(solution)/shard_map/all_gather | solution.py:54
Sparse Core Ops, SparseCore 0:
  20.6 136.4 all-reduce.2
  163.9 52.5 all-gather.1
where the time goes:
time: 226 us
  waiting for transfers between devices  187 us (83%)
  between operations  15 us (7%)
  other arithmetic  9.86 us (4%)
  local copies, waits for them, and re-layouts  9.78 us (4%)
  matrix products  4.35 us (2%)
    psum x1, waiting for transfers between devices, body(): summed = lax.psum(term.reshape(taps, -1), 'dp')  137 us
    all_gather x1, waiting for transfers between devices, body(): lax.all_gather(new_master.astype(jnp.bfloat16), 'dp', axis=1, tiled=True)  50.2 us
    unnamed x26, local copies, waits for them, and re-layouts  6.44 us
  transfers between devices with their start and end apart: 2, of which 2 were waited for; matrix products, arithmetic and copies ran while one was open for 1% of the time, Pallas kernels for 0%

commit v1 on v0

--- a/solution.py
+++ b/solution.py
@@ -1,7 +1,16 @@
+import functools
+
 import jax
 import jax.numpy as jnp
 from jax import lax
+from jax.experimental import pallas as pl
+from jax.experimental.pallas import tpu as pltpu
 from jax.sharding import PartitionSpec as P
+
+MESH = pl.DeviceIdType.MESH
+LANES = 128
+F32 = jnp.float32
+BF16 = jnp.bfloat16
 
 
 def norm_act(pre, gain, bias):
@@ -35,29 +44,331 @@
     return (windows, dpre, jnp.concatenate([dinput, tail], axis=1))
 
 
-def body(
+def adamw(grad, scale, master, first_moment, second_moment):
+    clipped = scale * grad
+    new_first = 0.9 * first_moment + 0.1 * clipped
+    new_second = 0.999 * second_moment + 0.001 * clipped * clipped
+    update = new_first / (1.0 - 0.9**20) / (jnp.sqrt(new_second / (1.0 - 0.999**20)) + 1e-08)
+    new_master = master - 0.0001 * (update + 0.01 * master)
+    return update, new_master, new_first, new_second
+
+
+def plain_body(
     inputs, weights, ln_gain, ln_bias, projection, targets, master, first_moment, second_moment
 ):
     windows, dpre, input_grad = local_pass(inputs, weights, ln_gain, ln_bias, projection, targets)
     taps = weights.shape[0]
     term = jnp.einsum("bfo,bfki->koi", dpre, windows, preferred_element_type=jnp.float32)
-    summed = lax.psum(term.reshape(taps, -1), "dp")
-    squares = jnp.sum(summed * summed)
-    width = master.shape[1]
-    grad = lax.dynamic_slice_in_dim(summed, lax.axis_index("dp") * width, width, 1)
+    grad = lax.psum_scatter(term.reshape(taps, -1), "dp", scatter_dimension=1, tiled=True)
+    squares = lax.psum(jnp.sum(grad * grad), "dp")
     scale = jnp.minimum(1.0, 1.0 / (jnp.sqrt(squares) + 1e-06))
-    clipped = scale * grad
-    new_first = 0.9 * first_moment + 0.1 * clipped
-    new_second = 0.999 * second_moment + 0.001 * clipped * clipped
-    update = new_first / (1.0 - 0.9**20) / (jnp.sqrt(new_second / (1.0 - 0.999**20)) + 1e-08)
-    new_master = master - 0.0001 * (update + 0.01 * master)
+    update, new_master, new_first, new_second = adamw(
+        grad, scale, master, first_moment, second_moment
+    )
     new_weights = lax.all_gather(new_master.astype(jnp.bfloat16), "dp", axis=1, tiled=True)
     return (input_grad, update, new_master, new_first, new_second, new_weights)
 
 
+def dot(a, b, dims):
+    return lax.dot_general(a, b, (dims, ((), ())), preferred_element_type=F32)
+
+
+def step_kernel(
+    n, frames_out,
+    inputs, kern, gain_ref, bias_ref, projection, targets, master, first, second,
+    dinput, update, new_master, new_first, new_second, gathered,
+    frames32, win, slope, normed, dpre_ref, term,
+    out0, in0, out1, in1, out2, in2, out3, in3, sq_out, sq_in, grad,
+    s0, r0, s1, r1, s2, r2, s3, r3, sq_s, sq_r, zs_s, zs_r, xs, xr, ys, yr, dxs, dxr, dys, dyr,
+    cs, cr,
+):
+    clips, frames_in, chans = inputs.shape
+    tiles = chans // LANES
+    fpad = win.shape[1] // clips
+    rows = grad.shape[1] // chans
+    width = grad.shape[1]
+    depth = n // 8
+
+    me = lax.axis_index("dp")
+    c = me % 2
+    x = (me // 2) % 2
+    y = (me // 4) % 2
+    z = me // 8
+    core_peer = me + 1 - 2 * c
+    x_peer = me + 2 - 4 * x
+    y_peer = me + 4 - 8 * y
+
+    barrier = pltpu.get_barrier_semaphore()
+    for j in range(1, n):
+        pl.semaphore_signal(barrier, inc=1, device_id=((me + j) % n,), device_id_type=MESH)
+
+    for b in range(clips):
+        for l in range(tiles):
+            lanes = slice(l * LANES, (l + 1) * LANES)
+            frames32[b, l, 0:frames_in, :] = inputs[b, :, lanes].astype(F32)
+            frames32[b, l, 2 * frames_out : 2 * fpad, :] = jnp.zeros(
+                (2 * fpad - 2 * frames_out, LANES), F32
+            )
+            for t in range(2):
+                win[t, b * fpad : (b + 1) * fpad, lanes] = frames32[
+                    b, l, pl.ds(t, fpad, stride=2), :
+                ].astype(BF16)
+
+    gain = gain_ref[...]
+    bias = bias_ref[...]
+    live = lax.broadcasted_iota(jnp.int32, (fpad, 1), 0) < frames_out
+    means = []
+    invs = []
+    for b in range(clips):
+        part = slice(b * fpad, (b + 1) * fpad)
+        pre = dot(win[0, part, :], kern[0], ((1,), (1,))) + dot(
+            win[1, part, :], kern[1], ((1,), (1,))
+        )
+        center = pre - jnp.mean(pre, axis=-1, keepdims=True)
+        spread = jnp.mean(center * center, axis=-1, keepdims=True)
+        inv = lax.rsqrt(spread + 1e-05)
+        nrm = center * inv
+        h = nrm * gain + bias
+        cdf = 0.5 + 0.5 * lax.erf(h * (0.5**0.5))
+        act = jnp.where(live, h * cdf, 0.0)
+        pdf = jnp.exp(-0.5 * h * h) * 0.3989422804014327
+        slope[part, :] = jnp.where(live, (cdf + h * pdf) * gain, 0.0)
+        normed[part, :] = nrm
+        means.append(jnp.sum(act, axis=0, keepdims=True) / frames_out)
+        invs.append(inv)
+    pooled = jnp.concatenate(means, axis=0).astype(BF16)
+    predicted = dot(pooled, projection[...], ((1,), (0,)))
+    miss = (predicted - targets[...]).astype(BF16)
+    back = dot(miss, projection[...], ((1,), (1,))) / frames_out
+    for b in range(clips):
+        part = slice(b * fpad, (b + 1) * fpad)
+        nrm = normed[part, :]
+        dn = slope[part, :] * back[b : b + 1, :]
+        low = jnp.mean(dn, axis=-1, keepdims=True)
+        tilt = jnp.mean(dn * nrm, axis=-1, keepdims=True)
+        dpre_ref[part, :] = (invs[b] * (dn - low - nrm * tilt)).astype(BF16)
+
+    for t in range(2):
+        for half in range(2):
+            span = chans // 2
+            value = dot(
+                dpre_ref[:, half * span : (half + 1) * span], win[t], ((0,), (0,))
+            )
+            for k in range(span // rows):
+                d = half * (span // rows) + k
+                term[d % 2, t, (d // 2) % 2, (d // 4) % 2, d // 8] = value[
+                    k * rows : (k + 1) * rows, :
+                ]
+
+    def send(src, dst, ssem, rsem, peer):
+        copy = pltpu.make_async_remote_copy(
+            src_ref=src, dst_ref=dst, send_sem=ssem, recv_sem=rsem,
+            device_id=(peer,), device_id_type=MESH,
+        )
+        copy.start()
+        return copy
+
+    def input_grad(t):
+        value = dot(dpre_ref[...], kern[t], ((1,), (0,)))
+        for b in range(clips):
+            for l in range(tiles):
+                frames32[b, l, pl.ds(t, fpad, stride=2), :] = value[
+                    b * fpad : (b + 1) * fpad, l * LANES : (l + 1) * LANES
+                ]
+
+    pl.semaphore_wait(barrier, n - 1)
+
+    out0[...] = term[1 - c].astype(BF16)
+    copy0 = send(out0, in0, s0, r0, core_peer)
+    input_grad(0)
+    copy0.wait()
+    out1[0] = (term[c, 0, 1 - x] + in0[0, 1 - x].astype(F32)).astype(BF16)
+    copy1x = send(out1.at[0], in1.at[0], s1.at[0], r1.at[0], x_peer)
+    out1[1] = (term[c, 1, :, 1 - y] + in0[1, :, 1 - y].astype(F32)).astype(BF16)
+    copy1y = send(out1.at[1], in1.at[1], s1.at[1], r1.at[1], y_peer)
+    input_grad(1)
+    copy1x.wait()
+    copy1y.wait()
+    out2[0] = (
+        term[c, 0, x, 1 - y] + in0[0, x, 1 - y].astype(F32) + in1[0, 1 - y].astype(F32)
+    ).astype(BF16)
+    copy2y = send(out2.at[0], in2.at[0], s2.at[0], r2.at[0], y_peer)
+    out2[1] = (
+        term[c, 1, 1 - x, y] + in0[1, 1 - x, y].astype(F32) + in1[1, 1 - x].astype(F32)
+    ).astype(BF16)
+    copy2x = send(out2.at[1], in2.at[1], s2.at[1], r2.at[1], x_peer)
+    for b in range(clips):
+        for l in range(tiles):
+            dinput[b, :, l * LANES : (l + 1) * LANES] = frames32[b, l, 0:frames_in, :].astype(BF16)
+    copy2y.wait()
+    copy2x.wait()
+
+    def held(t, zz):
+        return (
+            term[c, t, x, y, zz]
+            + in0[t, x, y, zz].astype(F32)
+            + in1[t, y if t == 0 else x, zz].astype(F32)
+            + in2[t, zz].astype(F32)
+        )
+
+    copies3 = []
+    for j in range(1, depth):
+        zz = (z + j) % depth
+        for t in range(2):
+            out3[j - 1, t] = held(t, zz).astype(BF16)
+        copies3.append(
+            send(out3.at[j - 1], in3.at[j - 1], s3.at[j - 1], r3.at[j - 1], (me + 8 * j) % n)
+        )
+    own = [held(t, z) for t in range(2)]
+    for j in range(1, depth):
+        copies3[j - 1].wait()
+        own = [own[t] + in3[j - 1, t].astype(F32) for t in range(2)]
+
+    squares = own[0] * own[0] + own[1] * own[1]
+    fold = sum(squares[:, l * LANES : (l + 1) * LANES] for l in range(tiles))
+    fold = sum(fold[k * 8 : (k + 1) * 8, :] for k in range(rows // 8))
+    sq_out[...] = fold
+    copies = []
+    for j in range(1, n):
+        copies.append(
+            send(sq_out, sq_in.at[j - 1], sq_s.at[j - 1], sq_r.at[j - 1], (me + j) % n)
+        )
+    for r in range(rows):
+        for t in range(2):
+            grad[t : t + 1, r * chans : (r + 1) * chans] = own[t][r : r + 1, :]
+    for copy in copies:
+        copy.wait()
+    total = jnp.sum(fold + jnp.sum(sq_in[...], axis=0))
+    scale = jnp.minimum(1.0, 1.0 / (jnp.sqrt(jnp.full((1, 1), total)) + 1e-06))
+
+    upd, nm, nf, ns = adamw(grad[...], scale, master[...], first[...], second[...])
+    update[...] = upd
+    new_master[...] = nm
+    new_first[...] = nf
+    new_second[...] = ns
+
+    def piece(zz, yy, xx, half=None):
+        start = (((zz * 2 + yy) * 2 + xx) * 2 + c) * width
+        size = width
+        if half is not None:
+            size = width // 2
+            start = start + half * size
+        return gathered.at[:, pl.ds(pl.multiple_of(start, LANES), size)]
+
+    mine = piece(z, y, x)
+    mine[...] = nm.astype(BF16)
+
+    pending = []
+    arrive = []
+    for j in range(1, depth):
+        copy = send(mine, mine, zs_s.at[j - 1], zs_r.at[j - 1], (me + 8 * j) % n)
+        arrive.append(copy)
+    fx, fy = [], []
+    for j in range(depth):
+        zz = (z + depth - j) % depth
+        if j:
+            arrive[j - 1].wait()
+        block = piece(zz, y, x)
+        fx.append(send(block, block, xs.at[j], xr.at[j], x_peer))
+        fy.append(send(block, block, ys.at[j], yr.at[j], y_peer))
+        pending.append(send(block, block, cs.at[4 * j], cr.at[4 * j], core_peer))
+    ex, ey = [], []
+    for j in range(depth):
+        zz = (z + depth - j) % depth
+        fy[j].wait()
+        block = piece(zz, 1 - y, x)
+        half = piece(zz, 1 - y, x, 0)
+        ex.append(send(half, half, dxs.at[j], dxr.at[j], x_peer))
+        pending.append(send(block, block, cs.at[4 * j + 1], cr.at[4 * j + 1], core_peer))
+        fx[j].wait()
+        block = piece(zz, y, 1 - x)
+        half = piece(zz, y, 1 - x, 1)
+        ey.append(send(half, half, dys.at[j], dyr.at[j], y_peer))
+        pending.append(send(block, block, cs.at[4 * j + 2], cr.at[4 * j + 2], core_peer))
+    for j in range(depth):
+        zz = (z + depth - j) % depth
+        ex[j].wait()
+        ey[j].wait()
+        block = piece(zz, 1 - y, 1 - x)
+        pending.append(send(block, block, cs.at[4 * j + 3], cr.at[4 * j + 3], core_peer))
+    for copy in pending:
+        copy.wait()
+
+
+def kernel_body(
+    n, inputs, weights, ln_gain, ln_bias, projection, targets, master, first_moment, second_moment
+):
+    clips, frames_in, chans = inputs.shape
+    taps = weights.shape[0]
+    frames_out = (frames_in - taps) // taps + 1
+    width = master.shape[1]
+    rows = width // chans
+    depth = n // 8
+    fpad = -(-(frames_in + 1) // 2 // 8) * 8
+    dma = pltpu.SemaphoreType.DMA
+    block = (depth, rows, chans)
+    piece = jax.ShapeDtypeStruct(master.shape, F32)
+    vmem = pl.BlockSpec(memory_space=pltpu.VMEM)
+    return pl.pallas_call(
+        functools.partial(step_kernel, n, frames_out),
+        out_shape=(
+            jax.ShapeDtypeStruct(inputs.shape, BF16),
+            piece,
+            piece,
+            piece,
+            piece,
+            jax.ShapeDtypeStruct(weights.shape, BF16),
+        ),
+        in_specs=[vmem] * 9,
+        out_specs=[vmem] * 6,
+        scratch_shapes=[
+            pltpu.VMEM((clips, chans // LANES, 2 * fpad, LANES), F32),
+            pltpu.VMEM((2, clips * fpad, chans), BF16),
+            pltpu.VMEM((clips * fpad, chans), F32),
+            pltpu.VMEM((clips * fpad, chans), F32),
+            pltpu.VMEM((clips * fpad, chans), BF16),
+            pltpu.VMEM((2, 2, 2, 2) + block, F32),
+            pltpu.VMEM((2, 2, 2) + block, BF16),
+            pltpu.VMEM((2, 2, 2) + block, BF16),
+            pltpu.VMEM((2, 2) + block, BF16),
+            pltpu.VMEM((2, 2) + block, BF16),
+            pltpu.VMEM((2,) + block, BF16),
+            pltpu.VMEM((2,) + block, BF16),
+            pltpu.VMEM((depth, 2, rows, chans), BF16),
+            pltpu.VMEM((depth, 2, rows, chans), BF16),
+            pltpu.VMEM((8, LANES), F32),
+            pltpu.VMEM((n - 1, 8, LANES), F32),
+            pltpu.VMEM(master.shape, F32),
+            dma, dma, dma((2,)), dma((2,)), dma((2,)), dma((2,)),
+            dma((depth,)), dma((depth,)), dma((n - 1,)), dma((n - 1,)),
+            dma((depth,)), dma((depth,)),
+            dma((depth,)), dma((depth,)), dma((depth,)), dma((depth,)),
+            dma((depth,)), dma((depth,)), dma((depth,)), dma((depth,)),
+            dma((4 * depth,)), dma((4 * depth,)),
+        ],
+        compiler_params=pltpu.CompilerParams(
+            collective_id=0, has_side_effects=True, vmem_limit_bytes=50 * 1024 * 1024
+        ),
+        name="conv_step",
+    )(
+        inputs, weights.reshape(taps, chans, chans), ln_gain[None], ln_bias[None], projection,
+        targets, master, first_moment, second_moment,
+    )
+
+
+def body(n, *args):
+    inputs, weights, master = args[0], args[1], args[6]
+    chans, width = inputs.shape[2], master.shape[1]
+    fits = (
+        n % 8 == 0 and n > 8 and weights.shape[0] == 2 and inputs.shape[1] % 2 == 1
+        and chans % (2 * LANES) == 0 and width % (16 * chans) == 0
+    )
+    return kernel_body(n, *args) if fits else plain_body(*args)
+
+
 def solution(mesh):
     return jax.shard_map(
-        body,
+        functools.partial(body, mesh.shape["dp"]),
         mesh=mesh,
         in_specs=(
             P("dp", None, None),

time: 226 us -> 50 us (0.22)
  waiting for transfers between devices: 187 us -> 0 us
  Pallas kernels: 0 us -> 41.7 us
  between operations: 15 us -> 0.7 us
  other arithmetic: 9.86 us -> 0 us
  matrix products: 4.35 us -> 0 us
  local copies, waits for them, and re-layouts: 9.78 us -> 7.42 us
    psum x1 -> x0, waiting for transfers between devices: 137 us -> none  [body(): summed = lax.psum(term.reshape(taps, -1), 'dp')]
    all_gather x1 -> x0, waiting for transfers between devices: 50.2 us -> none  [body(): lax.all_gather(new_master.astype(jnp.bfloat16), 'dp', axis=1, tiled=True)]
    pallas_call x0 -> x1, Pallas kernels: none -> 41.7 us  [kernel_body(): pl.pallas_call(functools.partial(step_kernel, n, frames_out), out_shape=(...]
    reduce_sum x5 -> x0, other arithmetic: 8.04 us -> none  [the longest x1 3.99 us: body(): squares = jnp.sum(summed * summed)]
    dot_general x4 -> x0, matrix products: 4.35 us -> none  [the longest x1 2.29 us: local_pass(): jnp.einsum('bfki,koi->bfo', windows, kernel, preferred_element_type=jnp.f...]
    unnamed x26 -> x21, local copies, waits for them, and re-layouts: 6.44 us -> 6.11 us
  transfers between devices with their start and end apart: 2 -> 0, of which waited for: 2 -> 0; matrix products, arithmetic and copies ran while one was open for 1% -> 0% of each run, Pallas kernels for 0% -> 0%
where the time goes in v1:
time: 50 us; the launch traced here: 49.9 us
  Pallas kernels  41.7 us (83%)
  local copies, waits for them, and re-layouts  7.42 us (15%)
  between operations  0.7 us (1%)
    pallas_call x1, Pallas kernels, kernel_body(): pl.pallas_call(functools.partial(step_kernel, n, frames_out), out_shape=(...  41.7 us
    unnamed x21, local copies, waits for them, and re-layouts  6.11 us
    pallas_call x1, local copies, waits for them, and re-layouts, kernel_body(): pl.pallas_call(functools.partial(step_kernel, n, frames_out), out_shape=(...  1.31 us

profile of v1, /device:TPU:0, one launch (start us, length us, event | category | flops | bytes accessed | tf_op | source)
XLA Modules:
  0.0 49.9 jit_solution(12574238448381516012)
XLA Ops:
  0.6 0.0 copy-start.6
  0.6 1.4 %copy.15.inputs = bf16[4,199,512]{2,1,0:T(8,128)(2,1)S(1)} copy(bf16[4,199,512]{2,0,1:T(4,128)(2,1)} %param.9) | data formatting | bytes 1630208 | tf_op args[0]
  2.0 0.1 copy-done.6
  2.1 0.0 copy-start
  2.1 0.0 copy-start.1
  2.1 0.0 copy-start.2
  2.1 0.0 copy-start.3
  2.1 0.0 copy-start.4
  2.1 0.0 copy-start.5
  2.1 1.1 %copy.19 = bf16[1,2,512,512]{3,2,1,0:T(8,128)(2,1)} copy(bf16[1,2,512,512]{3,1,2,0:T(2,128)(2,1)S(1)} %bitcast.9) | data formatting | bytes 2097152
  3.3 0.0 copy-done
  3.3 0.0 copy-done.1
  3.3 0.0 copy-done.2
  3.3 0.0 copy-done.3
  3.3 0.0 copy-done.4
  3.3 0.0 copy-done.5
  3.3 41.7 %conv_step.1 = (bf16[4,199,512]{2,1,0:T(8,128)(2,1)S(1)}, f32[2,8192]{1,0:T(2,128)S(1)}, f32[2,8192]{1,0:T(2,128)S(1)}, f32[2,8192]{1,0:T(2,128)S(1)}, f32[2,819...) custom-call(bf16[4,199,512]{2,1,0:T(8,128)(2,1)S(1)} %copy.15.inputs, bf16[2,512,512]{2,1,0:T(8,128)(2,1)} %bitcast.8, ...), custom_call_target="tpu_custom_call" | custom-call | tf_op jit(solution)/shard_map/conv_step/pallas_call | solution.py:312
  45.1 1.3 %copy.16 = bf16[4,199,512]{2,0,1:T(4,128)(2,1)} copy(bf16[4,199,512]{2,1,0:T(8,128)(2,1)S(1)} %get-tuple-element.6) | data formatting | bytes 1630208 | tf_op jit(solution)/shard_map/conv_step/pallas_call | solution.py:312
  46.4 0.6 %copy.25 = f32[2,8192]{1,0:T(2,128)} copy(f32[2,8192]{1,0:T(2,128)S(1)} %get-tuple-element.19) | data formatting | bytes 131072
  47.0 0.6 %copy.26 = f32[2,8192]{1,0:T(2,128)} copy(f32[2,8192]{1,0:T(2,128)S(1)} %get-tuple-element.20) | data formatting | bytes 131072
  47.6 0.6 %copy.27 = f32[2,8192]{1,0:T(2,128)} copy(f32[2,8192]{1,0:T(2,128)S(1)} %get-tuple-element.21) | data formatting | bytes 131072
  48.3 0.6 %copy.28 = f32[2,8192]{1,0:T(2,128)} copy(f32[2,8192]{1,0:T(2,128)S(1)} %get-tuple-element.22) | data formatting | bytes 131072
  48.9 1.0 %copy.29 = bf16[2,262144]{1,0:T(2,128)(2,1)} copy(bf16[2,262144]{1,0:T(2,128)(2,1)S(1)} %get-tuple-element.23) | data formatting | bytes 2097152
Async XLA Ops:
  0.6 1.5 %copy-start.6 = (bf16[2,262144]{1,0:T(2,128)(2,1)S(1)}, bf16[2,262144]{1,0:T(2,128)(2,1)}, u32[]{:S(2)}) copy-start(bf16[2,262144]{1,0:T(2,128)(2,1)} %param.10) | copy-start | bytes 3145732
  2.1 1.2 %copy-start = (f32[2,8192]{1,0:T(2,128)S(1)}, f32[2,8192]{1,0:T(2,128)}, u32[]{:S(2)}) copy-start(f32[2,8192]{1,0:T(2,128)} %master.1) | copy-start | bytes 196612
  2.1 1.2 %copy-start.1 = (f32[2,8192]{1,0:T(2,128)S(1)}, f32[2,8192]{1,0:T(2,128)}, u32[]{:S(2)}) copy-start(f32[2,8192]{1,0:T(2,128)} %first.1) | copy-start | bytes 196612
  2.1 1.2 %copy-start.2 = (f32[2,8192]{1,0:T(2,128)S(1)}, f32[2,8192]{1,0:T(2,128)}, u32[]{:S(2)}) copy-start(f32[2,8192]{1,0:T(2,128)} %second.1) | copy-start | bytes 196612
  2.1 1.2 %copy-start.3 = (f32[4,1024]{1,0:T(4,128)S(1)}, f32[4,1024]{1,0:T(4,128)}, u32[]{:S(2)}) copy-start(f32[4,1024]{1,0:T(4,128)} %targets.1) | copy-start | bytes 49156
  2.1 1.2 %copy-start.4 = (f32[512]{0:T(512)S(1)}, f32[512]{0:T(512)}, u32[]{:S(2)}) copy-start(f32[512]{0:T(512)} %param.11) | copy-start | bytes 6148
  2.1 1.2 %copy-start.5 = (f32[512]{0:T(512)S(1)}, f32[512]{0:T(512)}, u32[]{:S(2)}) copy-start(f32[512]{0:T(512)} %param.12) | copy-start | bytes 6148

commit v2 on v1

v2 whole, which is shorter than its diff:
```python
import functools

import jax
import jax.numpy as jnp
from jax import lax
from jax.experimental import pallas as pl
from jax.experimental.pallas import tpu as pltpu
from jax.sharding import PartitionSpec as P

MESH = pl.DeviceIdType.MESH
LANES = 128
F32 = jnp.float32
BF16 = jnp.bfloat16


def norm_act(pre, gain, bias):
    center = pre - jnp.mean(pre, axis=-1, keepdims=True)
    spread = jnp.mean(center * center, axis=-1, keepdims=True)
    normed = center * lax.rsqrt(spread + 1e-05)
    return jax.nn.gelu(normed * gain + bias, approximate=False)


def local_pass(inputs, weights, ln_gain, ln_bias, projection, targets):
    clips, frames_in, chans = inputs.shape
    taps = weights.shape[0]
    frames_out = (frames_in - taps) // taps + 1
    windows = inputs[:, : frames_out * taps].reshape(clips, frames_out, taps, chans)
    kernel = weights.reshape(taps, chans, chans)
    pre = jnp.einsum("bfki,koi->bfo", windows, kernel, preferred_element_type=jnp.float32)
    act, pull = jax.vjp(lambda value: norm_act(value, ln_gain, ln_bias), pre)
    pooled = jnp.mean(act, axis=1).astype(jnp.bfloat16)
    predicted = jnp.dot(pooled, projection, preferred_element_type=jnp.float32)
    miss = (predicted - targets).astype(jnp.bfloat16)
    back = lax.dot_general(
        miss, projection, (((1,), (1,)), ((), ())), preferred_element_type=jnp.float32
    )
    upstream = jnp.broadcast_to(back[:, None, :] / frames_out, act.shape)
    dpre = pull(upstream)[0].astype(jnp.bfloat16)
    dwin = jnp.einsum("bfo,koi->bfki", dpre, kernel, preferred_element_type=jnp.float32).astype(
        jnp.bfloat16
    )
    dinput = dwin.reshape(clips, frames_out * taps, chans)
    tail = jnp.zeros((clips, frames_in - frames_out * taps, chans), jnp.bfloat16)
    return (windows, dpre, jnp.concatenate([dinput, tail], axis=1))


def adamw(grad, scale, master, first_moment, second_moment):
    clipped = scale * grad
    new_first = 0.9 * first_moment + 0.1 * clipped
    new_second = 0.999 * second_moment + 0.001 * clipped * clipped
    update = new_first / (1.0 - 0.9**20) / (jnp.sqrt(new_second / (1.0 - 0.999**20)) + 1e-08)
    new_master = master - 0.0001 * (update + 0.01 * master)
    return update, new_master, new_first, new_second


def plain_body(
    inputs, weights, ln_gain, ln_bias, projection, targets, master, first_moment, second_moment
):
    windows, dpre, input_grad = local_pass(inputs, weights, ln_gain, ln_bias, projection, targets)
    taps = weights.shape[0]
    term = jnp.einsum("bfo,bfki->koi", dpre, windows, preferred_element_type=jnp.float32)
    grad = lax.psum_scatter(term.reshape(taps, -1), "dp", scatter_dimension=1, tiled=True)
    squares = lax.psum(jnp.sum(grad * grad), "dp")
    scale = jnp.minimum(1.0, 1.0 / (jnp.sqrt(squares) + 1e-06))
    update, new_master, new_first, new_second = adamw(
        grad, scale, master, first_moment, second_moment
    )
    new_weights = lax.all_gather(new_master.astype(jnp.bfloat16), "dp", axis=1, tiled=True)
    return (input_grad, update, new_master, new_first, new_second, new_weights)


def dot(a, b, dims):
    return lax.dot_general(a, b, (dims, ((), ())), preferred_element_type=F32)


def step_kernel(
    n, frames_out,
    inputs_hbm, weights_hbm, gain_ref, bias_ref, projection_hbm, targets, master_hbm, first_hbm,
    second_hbm,
    dinput, update, new_master, new_first, new_second, gathered,
    inputs, weights, projection, master, first, second,
    win, kern, pre_ref, slope, dpre_ref, dwin, term,
    out0, in0, out1, in1, out2, in2, out3, in3, sq_out, sq_in, grad,
    load, s0, r0, s1, r1, s2, r2, s3, r3, sq_s, sq_r,
    zs_s, zs_r, xs, xr, ys, yr, dxs, dxr, dys, dyr, cs, cr,
):
    frames_in, clips, chans = inputs.shape
    live_rows = frames_out * clips
    pad_rows = win.shape[0]
    width = grad.shape[1]
    rows = width // chans
    depth = n // 8

    me = lax.axis_index("dp")
    c = me % 2
    x = (me // 2) % 2
    y = (me // 4) % 2
    z = me // 8
    core_peer = me + 1 - 2 * c
    x_peer = me + 2 - 4 * x
    y_peer = me + 4 - 8 * y

    loads = [
        pltpu.make_async_copy(src, dst, load.at[k])
        for k, (src, dst) in enumerate(
            (
                (inputs_hbm, inputs), (weights_hbm, weights), (projection_hbm, projection),
                (master_hbm, master), (first_hbm, first), (second_hbm, second),
            )
        )
    ]
    for copy in loads:
        copy.start()

    barrier = pltpu.get_barrier_semaphore()
    for j in range(1, n):
        pl.semaphore_signal(barrier, inc=1, device_id=((me + j) % n,), device_id_type=MESH)

    loads[0].wait()
    pairs = inputs[0 : 2 * frames_out].reshape(frames_out, 2, clips, chans)
    for t in range(2):
        win[0:live_rows, t * chans : (t + 1) * chans] = (
            pairs[:, t].astype(F32).reshape(live_rows, chans).astype(BF16)
        )
    if pad_rows > live_rows:
        win[live_rows:pad_rows, :] = jnp.zeros((pad_rows - live_rows, 2 * chans), BF16)
    loads[1].wait()
    for q in range(chans // 16):
        flat = weights[:, q * 16 * chans : (q + 1) * 16 * chans].astype(F32)
        flat = flat.reshape(2, 16, chans)
        for t in range(2):
            kern[q * 16 : (q + 1) * 16, t * chans : (t + 1) * chans] = flat[t].astype(BF16)

    pre_ref[...] = dot(win[...], kern[...], ((1,), (1,)))
    gain = gain_ref[...]
    bias = bias_ref[...]
    step = 80 if pad_rows % 80 == 0 else 16
    fold = jnp.zeros((8, chans), F32)
    invs = []
    for base in range(0, pad_rows, step):
        part = slice(base, base + step)
        pre = pre_ref[part, :]
        center = pre - jnp.mean(pre, axis=-1, keepdims=True)
        spread = jnp.mean(center * center, axis=-1, keepdims=True)
        inv = lax.rsqrt(spread + 1e-05)
        nrm = center * inv
        h = nrm * gain + bias
        cdf = 0.5 + 0.5 * lax.erf(h * (0.5**0.5))
        pdf = jnp.exp(-0.5 * h * h) * 0.3989422804014327
        act = h * cdf
        rise = (cdf + h * pdf) * gain
        if base + step > live_rows:
            live = lax.broadcasted_iota(jnp.int32, (step, 1), 0) < live_rows - base
            act = jnp.where(live, act, 0.0)
            rise = jnp.where(live, rise, 0.0)
        slope[part, :] = rise
        pre_ref[part, :] = nrm
        fold = fold + jnp.sum(act.reshape(step // 8, 8, chans), axis=0)
        invs.append(inv)
    pooled = fold
    for k in range(1, 8 // clips):
        pooled = pooled + pltpu.roll(fold, k * clips, 0)
    pooled = (pooled / frames_out).astype(BF16)
    loads[2].wait()
    predicted = dot(pooled, projection[...], ((1,), (0,)))
    goal = jnp.concatenate([targets[...]] * (8 // clips), axis=0)
    miss = (predicted - goal).astype(BF16)
    back = dot(miss, projection[...], ((1,), (1,))) / frames_out
    for k, base in enumerate(range(0, pad_rows, step)):
        part = slice(base, base + step)
        nrm = pre_ref[part, :]
        dn = (slope[part, :].reshape(step // 8, 8, chans) * back[None]).reshape(step, chans)
        low = jnp.mean(dn, axis=-1, keepdims=True)
        tilt = jnp.mean(dn * nrm, axis=-1, keepdims=True)
        dpre_ref[part, :] = (invs[k] * (dn - low - nrm * tilt)).astype(BF16)

    span = chans // 2
    for half in range(2):
        value = dot(dpre_ref[:, half * span : (half + 1) * span], win[...], ((0,), (0,)))
        for k in range(span // rows):
            d = half * (span // rows) + k
            for t in range(2):
                term[d % 2, d // 8, t, (d // 2) % 2, (d // 4) % 2] = value[
                    k * rows : (k + 1) * rows, t * chans : (t + 1) * chans
                ]

    sent = []

    def send(src, dst, ssem, rsem, peer):
        copy = pltpu.make_async_remote_copy(
            src_ref=src, dst_ref=dst, send_sem=ssem, recv_sem=rsem,
            device_id=(peer,), device_id_type=MESH,
        )
        copy.start()
        sent.append(copy)
        return copy

    pl.semaphore_wait(barrier, n - 1)

    order = [(z + j) % depth for j in range(1, depth)] + [z]
    copies0 = []
    for k, zz in enumerate(order):
        out0[zz] = term[1 - c, zz].astype(BF16)
        copies0.append(send(out0.at[zz], in0.at[zz], s0.at[k], r0.at[k], core_peer))
    copies1 = []
    for k, zz in enumerate(order):
        copies0[k].wait_recv()
        out1[zz, 0] = (term[c, zz, 0, 1 - x] + in0[zz, 0, 1 - x].astype(F32)).astype(BF16)
        by_x = send(out1.at[zz, 0], in1.at[zz, 0], s1.at[2 * k], r1.at[2 * k], x_peer)
        out1[zz, 1] = (term[c, zz, 1, :, 1 - y] + in0[zz, 1, :, 1 - y].astype(F32)).astype(BF16)
        by_y = send(out1.at[zz, 1], in1.at[zz, 1], s1.at[2 * k + 1], r1.at[2 * k + 1], y_peer)
        copies1.append((by_x, by_y))
    dwin[...] = dot(dpre_ref[...], kern[...], ((1,), (0,)))

    def held(t, zz):
        return (
            term[c, zz, t, x, y]
            + in0[zz, t, x, y].astype(F32)
            + in1[zz, t, y if t == 0 else x].astype(F32)
            + in2[zz, t].astype(F32)
        )

    copies2, copies3 = [], []

    def to_z(k):
        copies2[k][0].wait_recv()
        copies2[k][1].wait_recv()
        for t in range(2):
            out3[k, t] = held(t, order[k]).astype(BF16)
        copies3.append(
            send(out3.at[k], in3.at[k], s3.at[k], r3.at[k], (me + 8 * (k + 1)) % n)
        )

    for k, zz in enumerate(order):
        copies1[k][0].wait_recv()
        copies1[k][1].wait_recv()
        out2[zz, 0] = (
            term[c, zz, 0, x, 1 - y]
            + in0[zz, 0, x, 1 - y].astype(F32)
            + in1[zz, 0, 1 - y].astype(F32)
        ).astype(BF16)
        by_y = send(out2.at[zz, 0], in2.at[zz, 0], s2.at[2 * k], r2.at[2 * k], y_peer)
        out2[zz, 1] = (
            term[c, zz, 1, 1 - x, y]
            + in0[zz, 1, 1 - x, y].astype(F32)
            + in1[zz, 1, 1 - x].astype(F32)
        ).astype(BF16)
        by_x = send(out2.at[zz, 1], in2.at[zz, 1], s2.at[2 * k + 1], r2.at[2 * k + 1], x_peer)
        copies2.append((by_y, by_x))
        if k:
            to_z(k - 1)
    copies2[-1][0].wait_recv()
    copies2[-1][1].wait_recv()
    own = [held(t, z) for t in range(2)]
    for k in range(depth - 1):
        copies3[k].wait_recv()
        own = [own[t] + in3[k, t].astype(F32) for t in range(2)]

    squares = own[0] * own[0] + own[1] * own[1]
    fold = sum(squares[:, l * LANES : (l + 1) * LANES] for l in range(chans // LANES))
    fold = sum(fold[k * 8 : (k + 1) * 8, :] for k in range(rows // 8))
    sq_out[...] = fold
    norms = []
    for j in range(1, n):
        norms.append(
            send(sq_out, sq_in.at[j - 1], sq_s.at[j - 1], sq_r.at[j - 1], (me + j) % n)
        )
    for r in range(rows):
        for t in range(2):
            grad[t : t + 1, r * chans : (r + 1) * chans] = own[t][r : r + 1, :]
    for k in range(3, 6):
        loads[k].wait()
    taps = [
        dwin[0:live_rows, t * chans : (t + 1) * chans]
        .astype(BF16)
        .reshape(frames_out, 1, clips, chans)
        for t in range(2)
    ]
    dinput[0 : 2 * frames_out] = jnp.concatenate(taps, axis=1).reshape(
        2 * frames_out, clips, chans
    )
    if frames_in > 2 * frames_out:
        dinput[2 * frames_out : frames_in] = jnp.zeros(
            (frames_in - 2 * frames_out, clips, chans), BF16
        )
    for copy in norms:
        copy.wait_recv()
    total = jnp.sum(fold + jnp.sum(sq_in[...], axis=0))
    scale = jnp.minimum(1.0, 1.0 / (jnp.sqrt(jnp.full((1, 1), total)) + 1e-06))

    upd, nm, nf, ns = adamw(grad[...], scale, master[...], first[...], second[...])

    def piece(zz, yy, xx, half=None):
        start = (((zz * 2 + yy) * 2 + xx) * 2 + c) * width
        size = width
        if half is not None:
            size = width // 2
            start = start + half * size
        return gathered.at[:, pl.ds(pl.multiple_of(start, LANES), size)]

    mine = piece(z, y, x)
    mine[...] = nm.astype(BF16)

    arrive = []
    for j in range(1, depth):
        copy = send(mine, mine, zs_s.at[j - 1], zs_r.at[j - 1], (me + 8 * j) % n)
        arrive.append(copy)
    fx, fy, cores = [], [], []
    for j in range(depth):
        zz = (z + depth - j) % depth
        if j:
            arrive[j - 1].wait_recv()
        block = piece(zz, y, x)
        fx.append(send(block, block, xs.at[j], xr.at[j], x_peer))
        fy.append(send(block, block, ys.at[j], yr.at[j], y_peer))
        cores.append(send(block, block, cs.at[4 * j], cr.at[4 * j], core_peer))
        if j == 0:
            update[...] = upd
            new_master[...] = nm
            new_first[...] = nf
            new_second[...] = ns
    ex, ey = [], []
    for j in range(depth):
        zz = (z + depth - j) % depth
        fy[j].wait_recv()
        block = piece(zz, 1 - y, x)
        half = piece(zz, 1 - y, x, 0)
        ex.append(send(half, half, dxs.at[j], dxr.at[j], x_peer))
        cores.append(send(block, block, cs.at[4 * j + 1], cr.at[4 * j + 1], core_peer))
        fx[j].wait_recv()
        block = piece(zz, y, 1 - x)
        half = piece(zz, y, 1 - x, 1)
        ey.append(send(half, half, dys.at[j], dyr.at[j], y_peer))
        cores.append(send(block, block, cs.at[4 * j + 2], cr.at[4 * j + 2], core_peer))
    for j in range(depth):
        zz = (z + depth - j) % depth
        ex[j].wait_recv()
        ey[j].wait_recv()
        block = piece(zz, 1 - y, 1 - x)
        cores.append(send(block, block, cs.at[4 * j + 3], cr.at[4 * j + 3], core_peer))
    for copy in cores:
        copy.wait_recv()
    for copy in sent:
        copy.wait_send()


def hand_over(*refs):
    count = (len(refs) - 1) // 2
    sems = refs[-1]
    copies = [
        pltpu.make_async_copy(refs[k], refs[count + k], sems.at[k]) for k in range(count)
    ]
    for copy in copies:
        copy.start()
    for copy in copies:
        copy.wait()


def kernel_body(
    n, inputs, weights, ln_gain, ln_bias, projection, targets, master, first_moment, second_moment
):
    clips, frames_in, chans = inputs.shape
    taps = weights.shape[0]
    frames_out = (frames_in - taps) // taps + 1
    width = master.shape[1]
    rows = width // chans
    depth = n // 8
    pad = -(-clips * frames_out // 16) * 16
    dma = pltpu.SemaphoreType.DMA
    block = (rows, chans)
    piece = jax.ShapeDtypeStruct(master.shape, F32)
    frames = jnp.transpose(inputs, (1, 0, 2))
    outs = (
        jax.ShapeDtypeStruct(frames.shape, BF16),
        piece,
        piece,
        piece,
        piece,
        jax.ShapeDtypeStruct(weights.shape, BF16),
    )
    vmem = pl.BlockSpec(memory_space=pltpu.VMEM)
    hbm = pl.BlockSpec(memory_space=pl.ANY)
    results = pl.pallas_call(
        functools.partial(step_kernel, n, frames_out),
        out_shape=outs,
        in_specs=[hbm, hbm, vmem, vmem, hbm, vmem, hbm, hbm, hbm],
        out_specs=[vmem] * 6,
        scratch_shapes=[
            pltpu.VMEM(frames.shape, BF16),
            pltpu.VMEM(weights.shape, BF16),
            pltpu.VMEM(projection.shape, BF16),
            pltpu.VMEM(master.shape, F32),
            pltpu.VMEM(master.shape, F32),
            pltpu.VMEM(master.shape, F32),
            pltpu.VMEM((pad, 2 * chans), BF16),
            pltpu.VMEM((chans, 2 * chans), BF16),
            pltpu.VMEM((pad, chans), F32),
            pltpu.VMEM((pad, chans), F32),
            pltpu.VMEM((pad, chans), BF16),
            pltpu.VMEM((pad, 2 * chans), F32),
            pltpu.VMEM((2, depth, 2, 2, 2) + block, F32),
            pltpu.VMEM((depth, 2, 2, 2) + block, BF16),
            pltpu.VMEM((depth, 2, 2, 2) + block, BF16),
            pltpu.VMEM((depth, 2, 2) + block, BF16),
            pltpu.VMEM((depth, 2, 2) + block, BF16),
            pltpu.VMEM((depth, 2) + block, BF16),
            pltpu.VMEM((depth, 2) + block, BF16),
            pltpu.VMEM((depth, 2) + block, BF16),
            pltpu.VMEM((depth, 2) + block, BF16),
            pltpu.VMEM((8, LANES), F32),
            pltpu.VMEM((n - 1, 8, LANES), F32),
            pltpu.VMEM(master.shape, F32),
            dma((6,)),
            dma((depth,)), dma((depth,)),
            dma((2 * depth,)), dma((2 * depth,)),
            dma((2 * depth,)), dma((2 * depth,)),
            dma((depth,)), dma((depth,)), dma((n - 1,)), dma((n - 1,)),
            dma((depth,)), dma((depth,)),
            dma((depth,)), dma((depth,)), dma((depth,)), dma((depth,)),
            dma((depth,)), dma((depth,)), dma((depth,)), dma((depth,)),
            dma((4 * depth,)), dma((4 * depth,)),
        ],
        compiler_params=pltpu.CompilerParams(
            collective_id=0, has_side_effects=True, vmem_limit_bytes=40 * 1024 * 1024
        ),
        name="conv_step",
    )(
        frames, weights, ln_gain[None], ln_bias[None], projection, targets, master, first_moment,
        second_moment,
    )
    results = pl.pallas_call(
        hand_over,
        out_shape=outs,
        in_specs=[hbm] * 6,
        out_specs=[hbm] * 6,
        scratch_shapes=[dma((6,))],
        name="hand_over",
    )(*results)
    return (jnp.transpose(results[0], (1, 0, 2)),) + tuple(results[1:])


def body(n, *args):
    inputs, weights, master = args[0], args[1], args[6]
    chans, width = inputs.shape[2], master.shape[1]
    fits = (
        n % 8 == 0 and n > 8 and weights.shape[0] == 2 and 8 % inputs.shape[0] == 0
        and chans % (2 * LANES) == 0 and width % (16 * chans) == 0
    )
    return kernel_body(n, *args) if fits else plain_body(*args)


def solution(mesh):
    return jax.shard_map(
        functools.partial(body, mesh.shape["dp"]),
        mesh=mesh,
        in_specs=(
            P("dp", None, None),
            P(),
            P(),
            P(),
            P(),
            P("dp", None),
            P(None, "dp"),
            P(None, "dp"),
            P(None, "dp"),
        ),
        out_specs=(
            P("dp", None, None),
            P(None, "dp"),
            P(None, "dp"),
            P(None, "dp"),
            P(None, "dp"),
            P(),
        ),
        check_vma=False,
    )
```

time: 50 us -> 118 us (2.36)
  Pallas kernels: 41.7 us -> 105 us
  local copies, waits for them, and re-layouts: 7.42 us -> 11.9 us
    pallas_call x1 -> x2, Pallas kernels: 41.7 us -> 105 us  [the longest x1 65.5 us: kernel_body(): pl.pallas_call(hand_over, out_shape=outs, in_specs=[hbm] * 6, out_specs=[...]
    unnamed x21 -> x30, local copies, waits for them, and re-layouts: 6.11 us -> 11.9 us
    pallas_call x1 -> x0, local copies, waits for them, and re-layouts: 1.31 us -> none  [kernel_body(): pl.pallas_call(functools.partial(step_kernel, n, frames_out), out_shape=(...]
where the time goes in v2:
time: 118 us; the launch traced here: 117 us
  Pallas kernels  105 us (89%)
  local copies, waits for them, and re-layouts  11.9 us (10%)
    pallas_call x1, Pallas kernels, kernel_body(): pl.pallas_call(hand_over, out_shape=outs, in_specs=[hbm] * 6, out_specs=[...  65.5 us
    pallas_call x1, Pallas kernels, kernel_body(): pl.pallas_call(functools.partial(step_kernel, n, frames_out), out_shape=o...  39.1 us
    unnamed x30, local copies, waits for them, and re-layouts  11.9 us

profile of v2, /device:TPU:0, one launch (start us, length us, event | category | flops | bytes accessed | tf_op | source)
XLA Modules:
  0.0 117.2 jit_solution(6940907859035582471)
XLA Ops:
  0.6 0.0 copy-start.14
  0.6 0.0 copy-start.13
  0.7 0.7 copy-done.14
  1.3 0.0 copy-done.13
  1.3 0.0 copy-start
  1.3 1.2 %copy-done = bf16[2,262144]{1,0:T(2,128)(2,1)S(1)} copy-done((bf16[2,262144]{1,0:T(2,128)(2,1)S(1)}, bf16[2,262144]{1,0:T(2,128)(2,1)}, u32[]{:S(2)}) %copy-start) | copy-done | bytes 1048600
  2.6 0.0 copy-start.1
  2.6 1.2 %copy-done.1 = bf16[512,1024]{1,0:T(8,128)(2,1)S(1)} copy-done((bf16[512,1024]{1,0:T(8,128)(2,1)S(1)}, bf16[512,1024]{1,0:T(8,128)(2,1)}, u32[]{:S(2)}) %copy-start.1) | copy-done | bytes 1048600
  3.8 0.0 copy-start.3
  3.8 1.1 copy-done.3
  4.9 0.0 copy-start.5
  4.9 0.8 copy-done.5
  5.8 0.0 copy-start.6
  5.8 0.8 copy-done.6
  6.6 0.0 copy-start.7
  6.6 0.8 copy-done.7
  7.4 0.0 copy-start.12
  7.5 0.7 copy-done.12
  8.2 39.1 %conv_step.1 = (bf16[199,4,512]{2,1,0:T(4,128)(2,1)S(1)}, f32[2,8192]{1,0:T(2,128)S(1)}, f32[2,8192]{1,0:T(2,128)S(1)}, f32[2,8192]{1,0:T(2,128)S(1)}, f32[2,819...) custom-call(bf16[199,4,512]{2,1,0:T(4,128)(2,1)S(1)} %bitcast.4, bf16[2,262144]{1,0:T(2,128)(2,1)S(1)} %copy-done, ...), custom_call_target="tpu_custom_call" | custom-call | tf_op jit(solution)/shard_map/conv_step/pallas_call | solution.py:383
  47.2 0.0 copy-start.2
  47.2 1.0 copy-done.2
  48.2 0.0 copy-start.4
  48.2 0.9 copy-done.4
  49.1 0.0 copy-start.8
  49.1 0.6 copy-done.8
  49.8 0.0 copy-start.9
  49.8 0.6 copy-done.9
  50.4 0.0 copy-start.10
  50.4 0.6 copy-done.10
  51.0 0.0 copy-start.11
  51.0 0.6 copy-done.11
  51.7 65.5 %hand_over.1 = (bf16[199,4,512]{2,1,0:T(4,128)(2,1)}, f32[2,8192]{1,0:T(2,128)}, f32[2,8192]{1,0:T(2,128)}, f32[2,8192]{1,0:T(2,128)}, f32[2,8192]{1,0:T(2,128)}, /*index=5*/bf16[2,262144]{1,0:T(2,128)(2,1)}) custom-call(bf16[199,4,512]{2,1,0:T(4,128)(2,1)} %copy-done.4, f32[2,8192]{1,0:T(2,128)} %copy-done.8, f32[2,8192]{1,0:T(2,128)} %copy-done.9, ...), custom_call_target="tpu_custom_call" | custom-call | tf_op jit(solution)/shard_map/hand_over/pallas_call | solution.py:431
Async XLA Ops:
  0.6 0.7 copy-start.14
  0.6 0.7 copy-start.13
  1.3 1.2 %copy-start = (bf16[2,262144]{1,0:T(2,128)(2,1)S(1)}, bf16[2,262144]{1,0:T(2,128)(2,1)}, u32[]{:S(2)}) copy-start(bf16[2,262144]{1,0:T(2,128)(2,1)} %weights_hbm.1) | copy-start | bytes 3145732
  2.6 1.2 %copy-start.1 = (bf16[512,1024]{1,0:T(8,128)(2,1)S(1)}, bf16[512,1024]{1,0:T(8,128)(2,1)}, u32[]{:S(2)}) copy-start(bf16[512,1024]{1,0:T(8,128)(2,1)} %projection_hbm.1) | copy-start | bytes 3145732
  3.8 1.1 copy-start.3
  4.9 0.8 copy-start.5
  5.8 0.8 copy-start.6
  6.6 0.8 copy-start.7
  7.4 0.7 copy-start.12
  47.2 1.0 copy-start.2
  48.2 0.9 copy-start.4
  49.1 0.6 copy-start.8
  49.8 0.6 copy-start.9
  50.4 0.6 copy-start.10
  51.0 0.6 copy-start.11

commit v3 on v2

--- a/solution.py
+++ b/solution.py
@@ -75,10 +75,10 @@
 
 def step_kernel(
     n, frames_out,
-    inputs_hbm, weights_hbm, gain_ref, bias_ref, projection_hbm, targets, master_hbm, first_hbm,
-    second_hbm,
+    inputs_hbm, weights_hbm, gain_hbm, bias_hbm, projection_hbm, targets_hbm, master_hbm,
+    first_hbm, second_hbm,
     dinput, update, new_master, new_first, new_second, gathered,
-    inputs, weights, projection, master, first, second,
+    inputs, weights, gain_ref, bias_ref, projection, targets, master, first, second,
     win, kern, pre_ref, slope, dpre_ref, dwin, term,
     out0, in0, out1, in1, out2, in2, out3, in3, sq_out, sq_in, grad,
     load, s0, r0, s1, r1, s2, r2, s3, r3, sq_s, sq_r,
@@ -104,7 +104,8 @@
         pltpu.make_async_copy(src, dst, load.at[k])
         for k, (src, dst) in enumerate(
             (
-                (inputs_hbm, inputs), (weights_hbm, weights), (projection_hbm, projection),
+                (inputs_hbm, inputs), (weights_hbm, weights), (gain_hbm, gain_ref),
+                (bias_hbm, bias_ref), (projection_hbm, projection), (targets_hbm, targets),
                 (master_hbm, master), (first_hbm, first), (second_hbm, second),
             )
         )
@@ -125,20 +126,26 @@
     if pad_rows > live_rows:
         win[live_rows:pad_rows, :] = jnp.zeros((pad_rows - live_rows, 2 * chans), BF16)
     loads[1].wait()
-    for q in range(chans // 16):
-        flat = weights[:, q * 16 * chans : (q + 1) * 16 * chans].astype(F32)
-        flat = flat.reshape(2, 16, chans)
+    group = 64 if chans % 64 == 0 else 16
+
+    @pl.loop(0, chans // group)
+    def _(q):
+        lanes = pl.ds(pl.multiple_of(q * group * chans, LANES), group * chans)
+        flat = weights[:, lanes].astype(F32).reshape(2, group, chans)
+        out = pl.ds(pl.multiple_of(q * group, group), group)
         for t in range(2):
-            kern[q * 16 : (q + 1) * 16, t * chans : (t + 1) * chans] = flat[t].astype(BF16)
+            kern[out, t * chans : (t + 1) * chans] = flat[t].astype(BF16)
 
     pre_ref[...] = dot(win[...], kern[...], ((1,), (1,)))
+    loads[2].wait()
+    loads[3].wait()
     gain = gain_ref[...]
     bias = bias_ref[...]
     step = 80 if pad_rows % 80 == 0 else 16
-    fold = jnp.zeros((8, chans), F32)
-    invs = []
-    for base in range(0, pad_rows, step):
-        part = slice(base, base + step)
+
+    def forward(i, fold):
+        base = pl.multiple_of(i * step, 16)
+        part = pl.ds(base, step)
         pre = pre_ref[part, :]
         center = pre - jnp.mean(pre, axis=-1, keepdims=True)
         spread = jnp.mean(center * center, axis=-1, keepdims=True)
@@ -147,42 +154,32 @@
         h = nrm * gain + bias
         cdf = 0.5 + 0.5 * lax.erf(h * (0.5**0.5))
         pdf = jnp.exp(-0.5 * h * h) * 0.3989422804014327
-        act = h * cdf
-        rise = (cdf + h * pdf) * gain
-        if base + step > live_rows:
-            live = lax.broadcasted_iota(jnp.int32, (step, 1), 0) < live_rows - base
-            act = jnp.where(live, act, 0.0)
-            rise = jnp.where(live, rise, 0.0)
-        slope[part, :] = rise
+        live = lax.broadcasted_iota(jnp.int32, (step, 1), 0) < live_rows - base
+        act = jnp.where(live, h * cdf, 0.0)
+        slope[part, :] = (cdf + h * pdf) * (gain * jnp.where(live, inv, 0.0))
         pre_ref[part, :] = nrm
-        fold = fold + jnp.sum(act.reshape(step // 8, 8, chans), axis=0)
-        invs.append(inv)
+        return fold + jnp.sum(act.reshape(step // 8, 8, chans), axis=0)
+
+    fold = lax.fori_loop(0, pad_rows // step, forward, jnp.zeros((8, chans), F32))
     pooled = fold
     for k in range(1, 8 // clips):
         pooled = pooled + pltpu.roll(fold, k * clips, 0)
     pooled = (pooled / frames_out).astype(BF16)
-    loads[2].wait()
+    loads[4].wait()
+    loads[5].wait()
     predicted = dot(pooled, projection[...], ((1,), (0,)))
     goal = jnp.concatenate([targets[...]] * (8 // clips), axis=0)
     miss = (predicted - goal).astype(BF16)
     back = dot(miss, projection[...], ((1,), (1,))) / frames_out
-    for k, base in enumerate(range(0, pad_rows, step)):
-        part = slice(base, base + step)
+
+    @pl.loop(0, pad_rows // step)
+    def _(i):
+        part = pl.ds(pl.multiple_of(i * step, 16), step)
         nrm = pre_ref[part, :]
         dn = (slope[part, :].reshape(step // 8, 8, chans) * back[None]).reshape(step, chans)
         low = jnp.mean(dn, axis=-1, keepdims=True)
         tilt = jnp.mean(dn * nrm, axis=-1, keepdims=True)
-        dpre_ref[part, :] = (invs[k] * (dn - low - nrm * tilt)).astype(BF16)
-
-    span = chans // 2
-    for half in range(2):
-        value = dot(dpre_ref[:, half * span : (half + 1) * span], win[...], ((0,), (0,)))
-        for k in range(span // rows):
-            d = half * (span // rows) + k
-            for t in range(2):
-                term[d % 2, d // 8, t, (d // 2) % 2, (d // 4) % 2] = value[
-                    k * rows : (k + 1) * rows, t * chans : (t + 1) * chans
-                ]
+        dpre_ref[part, :] = (dn - low - nrm * tilt).astype(BF16)
 
     sent = []
 
@@ -195,21 +192,40 @@
         sent.append(copy)
         return copy
 
-    pl.semaphore_wait(barrier, n - 1)
-
     order = [(z + j) % depth for j in range(1, depth)] + [z]
     copies0 = []
-    for k, zz in enumerate(order):
+    copies1 = []
+
+    def to_core(k):
+        zz = order[k]
+        span = chans // depth
+        value = dot(
+            dpre_ref[:, pl.ds(pl.multiple_of(zz * span, LANES), span)], win[...], ((0,), (0,))
+        )
+        for d in range(8):
+            for t in range(2):
+                term[d % 2, zz, t, (d // 2) % 2, d // 4] = value[
+                    d * rows : (d + 1) * rows, t * chans : (t + 1) * chans
+                ]
         out0[zz] = term[1 - c, zz].astype(BF16)
+        if k == 0:
+            pl.semaphore_wait(barrier, n - 1)
         copies0.append(send(out0.at[zz], in0.at[zz], s0.at[k], r0.at[k], core_peer))
-    copies1 = []
-    for k, zz in enumerate(order):
+
+    def to_near(k):
+        zz = order[k]
         copies0[k].wait_recv()
         out1[zz, 0] = (term[c, zz, 0, 1 - x] + in0[zz, 0, 1 - x].astype(F32)).astype(BF16)
         by_x = send(out1.at[zz, 0], in1.at[zz, 0], s1.at[2 * k], r1.at[2 * k], x_peer)
         out1[zz, 1] = (term[c, zz, 1, :, 1 - y] + in0[zz, 1, :, 1 - y].astype(F32)).astype(BF16)
         by_y = send(out1.at[zz, 1], in1.at[zz, 1], s1.at[2 * k + 1], r1.at[2 * k + 1], y_peer)
         copies1.append((by_x, by_y))
+
+    for k in range(depth):
+        to_core(k)
+        if k:
+            to_near(k - 1)
+    to_near(depth - 1)
     dwin[...] = dot(dpre_ref[...], kern[...], ((1,), (0,)))
 
     def held(t, zz):
@@ -268,7 +284,7 @@
     for r in range(rows):
         for t in range(2):
             grad[t : t + 1, r * chans : (r + 1) * chans] = own[t][r : r + 1, :]
-    for k in range(3, 6):
+    for k in range(6, 9):
         loads[k].wait()
     taps = [
         dwin[0:live_rows, t * chans : (t + 1) * chans]
@@ -378,17 +394,21 @@
         piece,
         jax.ShapeDtypeStruct(weights.shape, BF16),
     )
+    pin = lambda array: pltpu.with_memory_space_constraint(array, pltpu.HBM)
     vmem = pl.BlockSpec(memory_space=pltpu.VMEM)
-    hbm = pl.BlockSpec(memory_space=pl.ANY)
+    hbm = pl.BlockSpec(memory_space=pltpu.HBM)
     results = pl.pallas_call(
         functools.partial(step_kernel, n, frames_out),
         out_shape=outs,
-        in_specs=[hbm, hbm, vmem, vmem, hbm, vmem, hbm, hbm, hbm],
+        in_specs=[hbm] * 9,
         out_specs=[vmem] * 6,
         scratch_shapes=[
             pltpu.VMEM(frames.shape, BF16),
             pltpu.VMEM(weights.shape, BF16),
+            pltpu.VMEM((1, chans), F32),
+            pltpu.VMEM((1, chans), F32),
             pltpu.VMEM(projection.shape, BF16),
+            pltpu.VMEM(targets.shape, F32),
             pltpu.VMEM(master.shape, F32),
             pltpu.VMEM(master.shape, F32),
             pltpu.VMEM(master.shape, F32),
@@ -410,7 +430,7 @@
             pltpu.VMEM((8, LANES), F32),
             pltpu.VMEM((n - 1, 8, LANES), F32),
             pltpu.VMEM(master.shape, F32),
-            dma((6,)),
+            dma((9,)),
             dma((depth,)), dma((depth,)),
             dma((2 * depth,)), dma((2 * depth,)),
             dma((2 * depth,)), dma((2 * depth,)),
@@ -425,13 +445,18 @@
         ),
         name="conv_step",
     )(
-        frames, weights, ln_gain[None], ln_bias[None], projection, targets, master, first_moment,
-        second_moment,
+        *map(
+            pin,
+            (
+                frames, weights, ln_gain[None], ln_bias[None], projection, targets, master,
+                first_moment, second_moment,
+            ),
+        )
     )
     results = pl.pallas_call(
         hand_over,
         out_shape=outs,
-        in_specs=[hbm] * 6,
+        in_specs=[vmem] * 6,
         out_specs=[hbm] * 6,
         scratch_shapes=[dma((6,))],
         name="hand_over",
@@ -445,6 +470,7 @@
     fits = (
         n % 8 == 0 and n > 8 and weights.shape[0] == 2 and 8 % inputs.shape[0] == 0
         and chans % (2 * LANES) == 0 and width % (16 * chans) == 0
+        and chans % (LANES * (n // 8)) == 0
     )
     return kernel_body(n, *args) if fits else plain_body(*args)
 

time: 118 us -> 48.4 us (0.41)
  Pallas kernels: 105 us -> 43.2 us
  local copies, waits for them, and re-layouts: 11.9 us -> 4.35 us
    pallas_call x1, Pallas kernels: 65.5 us -> 2.96 us  [kernel_body(): pl.pallas_call(hand_over, out_shape=outs, in_specs=[vmem] * 6, out_specs=...]
    unnamed x30 -> x12, local copies, waits for them, and re-layouts: 11.9 us -> 4.35 us
where the time goes in v3:
time: 48.4 us; the launch traced here: 48.2 us
  Pallas kernels  43.2 us (89%)
  local copies, waits for them, and re-layouts  4.35 us (9%)
  between operations  0.66 us (1%)
    pallas_call x1, Pallas kernels, kernel_body(): pl.pallas_call(functools.partial(step_kernel, n, frames_out), out_shape=o...  40.2 us
    unnamed x12, local copies, waits for them, and re-layouts  4.35 us
    pallas_call x1, Pallas kernels, kernel_body(): pl.pallas_call(hand_over, out_shape=outs, in_specs=[vmem] * 6, out_specs=...  2.96 us

profile of v3, /device:TPU:0, one launch (start us, length us, event | category | flops | bytes accessed | tf_op | source)
XLA Modules:
  0.0 48.2 jit_solution(2296604060261307567)
XLA Ops:
  0.6 40.2 %conv_step.1 = (bf16[199,4,512]{2,1,0:T(4,128)(2,1)S(1)}, f32[2,8192]{1,0:T(2,128)S(1)}, f32[2,8192]{1,0:T(2,128)S(1)}, f32[2,8192]{1,0:T(2,128)S(1)}, f32[2,819...) custom-call(bf16[199,4,512]{2,1,0:T(4,128)(2,1)} %bitcast.4, bf16[2,262144]{1,0:T(2,128)(2,1)} %weights_hbm.1, ...), custom_call_target="tpu_custom_call" | custom-call | tf_op jit(solution)/shard_map/conv_step/pallas_call | solution.py:400
  40.9 0.0 copy-start
  40.9 1.0 %copy-done = bf16[2,262144]{1,0:T(2,128)(2,1)} copy-done((bf16[2,262144]{1,0:T(2,128)(2,1)}, bf16[2,262144]{1,0:T(2,128)(2,1)S(1)}, u32[]{:S(2)}) %copy-start) | copy-done | bytes 1048600
  41.8 0.0 copy-start.1
  41.8 0.9 %copy-done.1 = bf16[199,4,512]{2,1,0:T(4,128)(2,1)} copy-done((bf16[199,4,512]{2,1,0:T(4,128)(2,1)}, bf16[199,4,512]{2,1,0:T(4,128)(2,1)S(1)}, u32[]{:S(2)}) %copy-start.1) | copy-done | bytes 815128
  42.7 0.0 copy-start.2
  42.7 0.6 %copy-done.2 = f32[2,8192]{1,0:T(2,128)} copy-done((f32[2,8192]{1,0:T(2,128)}, f32[2,8192]{1,0:T(2,128)S(1)}, u32[]{:S(2)}) %copy-start.2) | copy-done | bytes 65560
  43.4 0.0 copy-start.3
  43.4 0.6 %copy-done.3 = f32[2,8192]{1,0:T(2,128)} copy-done((f32[2,8192]{1,0:T(2,128)}, f32[2,8192]{1,0:T(2,128)S(1)}, u32[]{:S(2)}) %copy-start.3) | copy-done | bytes 65560
  44.0 0.0 copy-start.4
  44.0 0.6 %copy-done.4 = f32[2,8192]{1,0:T(2,128)} copy-done((f32[2,8192]{1,0:T(2,128)}, f32[2,8192]{1,0:T(2,128)S(1)}, u32[]{:S(2)}) %copy-start.4) | copy-done | bytes 65560
  44.6 0.0 copy-start.5
  44.6 0.6 %copy-done.5 = f32[2,8192]{1,0:T(2,128)} copy-done((f32[2,8192]{1,0:T(2,128)}, f32[2,8192]{1,0:T(2,128)S(1)}, u32[]{:S(2)}) %copy-start.5) | copy-done | bytes 65560
  45.2 3.0 %hand_over.1 = (bf16[199,4,512]{2,1,0:T(4,128)(2,1)}, f32[2,8192]{1,0:T(2,128)}, f32[2,8192]{1,0:T(2,128)}, f32[2,8192]{1,0:T(2,128)}, f32[2,8192]{1,0:T(2,128)}, /*index=5*/bf16[2,262144]{1,0:T(2,128)(2,1)}) custom-call(bf16[199,4,512]{2,1,0:T(4,128)(2,1)} %copy-done.1, f32[2,8192]{1,0:T(2,128)} %copy-done.2, f32[2,8192]{1,0:T(2,128)} %copy-done.3, ...), custom_call_target="tpu_custom_call" | custom-call | tf_op jit(solution)/shard_map/hand_over/pallas_call | solution.py:456
Async XLA Ops:
  40.9 1.0 %copy-start = (bf16[2,262144]{1,0:T(2,128)(2,1)}, bf16[2,262144]{1,0:T(2,128)(2,1)S(1)}, u32[]{:S(2)}) copy-start(bf16[2,262144]{1,0:T(2,128)(2,1)S(1)} %get-tuple-element.23.refs_5_) | copy-start | bytes 3145732
  41.8 0.9 %copy-start.1 = (bf16[199,4,512]{2,1,0:T(4,128)(2,1)}, bf16[199,4,512]{2,1,0:T(4,128)(2,1)S(1)}, u32[]{:S(2)}) copy-start(bf16[199,4,512]{2,1,0:T(4,128)(2,1)S(1)} %get-tuple-element.18.refs_0_) | copy-start | bytes 2445316
  42.7 0.6 %copy-start.2 = (f32[2,8192]{1,0:T(2,128)}, f32[2,8192]{1,0:T(2,128)S(1)}, u32[]{:S(2)}) copy-start(f32[2,8192]{1,0:T(2,128)S(1)} %get-tuple-element.19.refs_1_) | copy-start | bytes 196612
  43.4 0.6 %copy-start.3 = (f32[2,8192]{1,0:T(2,128)}, f32[2,8192]{1,0:T(2,128)S(1)}, u32[]{:S(2)}) copy-start(f32[2,8192]{1,0:T(2,128)S(1)} %get-tuple-element.20.refs_2_) | copy-start | bytes 196612
  44.0 0.6 %copy-start.4 = (f32[2,8192]{1,0:T(2,128)}, f32[2,8192]{1,0:T(2,128)S(1)}, u32[]{:S(2)}) copy-start(f32[2,8192]{1,0:T(2,128)S(1)} %get-tuple-element.21.refs_3_) | copy-start | bytes 196612
  44.6 0.6 %copy-start.5 = (f32[2,8192]{1,0:T(2,128)}, f32[2,8192]{1,0:T(2,128)S(1)}, u32[]{:S(2)}) copy-start(f32[2,8192]{1,0:T(2,128)S(1)} %get-tuple-element.22.refs_4_) | copy-start | bytes 196612

commit v4 on v3

--- a/solution.py
+++ b/solution.py
@@ -274,12 +274,13 @@
 
     squares = own[0] * own[0] + own[1] * own[1]
     fold = sum(squares[:, l * LANES : (l + 1) * LANES] for l in range(chans // LANES))
-    fold = sum(fold[k * 8 : (k + 1) * 8, :] for k in range(rows // 8))
-    sq_out[...] = fold
+    sq_out[...] = jnp.sum(fold, axis=0, keepdims=True)
+    earlier = tuple(sent)
+    sent.clear()
     norms = []
     for j in range(1, n):
         norms.append(
-            send(sq_out, sq_in.at[j - 1], sq_s.at[j - 1], sq_r.at[j - 1], (me + j) % n)
+            send(sq_out, sq_in.at[pl.ds(j - 1, 1)], sq_s.at[j - 1], sq_r.at[j - 1], (me + j) % n)
         )
     for r in range(rows):
         for t in range(2):
@@ -299,9 +300,11 @@
         dinput[2 * frames_out : frames_in] = jnp.zeros(
             (frames_in - 2 * frames_out, clips, chans), BF16
         )
+    for copy in earlier:
+        copy.wait_send()
     for copy in norms:
         copy.wait_recv()
-    total = jnp.sum(fold + jnp.sum(sq_in[...], axis=0))
+    total = jnp.sum(sq_in[...]) + jnp.sum(sq_out[...])
     scale = jnp.minimum(1.0, 1.0 / (jnp.sqrt(jnp.full((1, 1), total)) + 1e-06))
 
     upd, nm, nf, ns = adamw(grad[...], scale, master[...], first[...], second[...])
@@ -335,6 +338,9 @@
             new_master[...] = nm
             new_first[...] = nf
             new_second[...] = ns
+            for copy in norms:
+                copy.wait_send()
+                sent.remove(copy)
     ex, ey = [], []
     for j in range(depth):
         zz = (z + depth - j) % depth
@@ -427,8 +433,8 @@
             pltpu.VMEM((depth, 2) + block, BF16),
             pltpu.VMEM((depth, 2) + block, BF16),
             pltpu.VMEM((depth, 2) + block, BF16),
-            pltpu.VMEM((8, LANES), F32),
-            pltpu.VMEM((n - 1, 8, LANES), F32),
+            pltpu.VMEM((1, LANES), F32),
+            pltpu.VMEM((n - 1, LANES), F32),
             pltpu.VMEM(master.shape, F32),
             dma((9,)),
             dma((depth,)), dma((depth,)),
@@ -459,6 +465,7 @@
         in_specs=[vmem] * 6,
         out_specs=[hbm] * 6,
         scratch_shapes=[dma((6,))],
+        compiler_params=pltpu.CompilerParams(vmem_limit_bytes=2 * 1024 * 1024),
         name="hand_over",
     )(*results)
     return (jnp.transpose(results[0], (1, 0, 2)),) + tuple(results[1:])

time: 48.4 us -> 41.2 us (0.85)
  local copies, waits for them, and re-layouts: 4.35 us -> 0 us
  Pallas kernels: 43.2 us -> 40.4 us
    unnamed x12 -> x0, local copies, waits for them, and re-layouts: 4.35 us -> none
    pallas_call x1, Pallas kernels: 2.96 us -> 1.38 us  [kernel_body(): pl.pallas_call(hand_over, out_shape=outs, in_specs=[vmem] * 6, out_specs=...]
    pallas_call x1, Pallas kernels: 40.2 us -> 39 us  [kernel_body(): pl.pallas_call(functools.partial(step_kernel, n, frames_out), out_shape=o...]
where the time goes in v4:
time: 41.2 us; the launch traced here: 41.1 us
  Pallas kernels  40.4 us (98%)
  between operations  0.64 us (2%)
    pallas_call x1, Pallas kernels, kernel_body(): pl.pallas_call(functools.partial(step_kernel, n, frames_out), out_shape=o...  39 us
    pallas_call x1, Pallas kernels, kernel_body(): pl.pallas_call(hand_over, out_shape=outs, in_specs=[vmem] * 6, out_specs=...  1.38 us

profile of v4, /device:TPU:0, one launch (start us, length us, event | category | flops | bytes accessed | tf_op | source)
XLA Modules:
  0.0 41.1 jit_solution(11738267088782374734)
XLA Ops:
  0.6 39.0 %conv_step.1 = (bf16[199,4,512]{2,1,0:T(4,128)(2,1)S(1)}, f32[2,8192]{1,0:T(2,128)S(1)}, f32[2,8192]{1,0:T(2,128)S(1)}, f32[2,8192]{1,0:T(2,128)S(1)}, f32[2,819...) custom-call(bf16[199,4,512]{2,1,0:T(4,128)(2,1)} %bitcast.4, bf16[2,262144]{1,0:T(2,128)(2,1)} %weights_hbm.1, ...), custom_call_target="tpu_custom_call" | custom-call | tf_op jit(solution)/shard_map/conv_step/pallas_call | solution.py:406
  39.7 1.4 %hand_over.1 = (bf16[199,4,512]{2,1,0:T(4,128)(2,1)}, f32[2,8192]{1,0:T(2,128)}, f32[2,8192]{1,0:T(2,128)}, f32[2,8192]{1,0:T(2,128)}, f32[2,8192]{1,0:T(2,128)}, /*index=5*/bf16[2,262144]{1,0:T(2,128)(2,1)}) custom-call(bf16[199,4,512]{2,1,0:T(4,128)(2,1)S(1)} %get-tuple-element.18.refs_0_, f32[2,8192]{1,0:T(2,128)S(1)} %get-tuple-element.19.refs_1_, ...), custom_call_target="tpu_custom_call" | custom-call | tf_op jit(solution)/shard_map/hand_over/pallas_call | solution.py:462

commit v5 on v4

--- a/solution.py
+++ b/solution.py
@@ -80,9 +80,8 @@
     dinput, update, new_master, new_first, new_second, gathered,
     inputs, weights, gain_ref, bias_ref, projection, targets, master, first, second,
     win, kern, pre_ref, slope, dpre_ref, dwin, term,
-    out0, in0, out1, in1, out2, in2, out3, in3, sq_out, sq_in, grad,
-    load, s0, r0, s1, r1, s2, r2, s3, r3, sq_s, sq_r,
-    zs_s, zs_r, xs, xr, ys, yr, dxs, dxr, dys, dyr, cs, cr,
+    out0, in0, out1, in1, out3, in3, sq_out, sq_in, grad,
+    load, s0, r0, s1, r1, s3, r3, sq_s, sq_r, zs_s, zs_r, near_s, near_r, cs, cr,
 ):
     frames_in, clips, chans = inputs.shape
     live_rows = frames_out * clips
@@ -99,6 +98,11 @@
     core_peer = me + 1 - 2 * c
     x_peer = me + 2 - 4 * x
     y_peer = me + 4 - 8 * y
+    near = (
+        (1 - x, 1 - y, x_peer + y_peer - me),
+        (1 - x, y, x_peer),
+        (x, 1 - y, y_peer),
+    )
 
     loads = [
         pltpu.make_async_copy(src, dst, load.at[k])
@@ -121,7 +125,7 @@
     pairs = inputs[0 : 2 * frames_out].reshape(frames_out, 2, clips, chans)
     for t in range(2):
         win[0:live_rows, t * chans : (t + 1) * chans] = (
-            pairs[:, t].astype(F32).reshape(live_rows, chans).astype(BF16)
+            pairs[:, t].reshape(live_rows, chans)
         )
     if pad_rows > live_rows:
         win[live_rows:pad_rows, :] = jnp.zeros((pad_rows - live_rows, 2 * chans), BF16)
@@ -131,10 +135,10 @@
     @pl.loop(0, chans // group)
     def _(q):
         lanes = pl.ds(pl.multiple_of(q * group * chans, LANES), group * chans)
-        flat = weights[:, lanes].astype(F32).reshape(2, group, chans)
+        flat = weights[:, lanes].reshape(2, group, chans)
         out = pl.ds(pl.multiple_of(q * group, group), group)
         for t in range(2):
-            kern[out, t * chans : (t + 1) * chans] = flat[t].astype(BF16)
+            kern[out, t * chans : (t + 1) * chans] = flat[t]
 
     pre_ref[...] = dot(win[...], kern[...], ((1,), (1,)))
     loads[2].wait()
@@ -204,7 +208,7 @@
         )
         for d in range(8):
             for t in range(2):
-                term[d % 2, zz, t, (d // 2) % 2, d // 4] = value[
+                term[d % 2, zz, (d // 2) % 2, d // 4, t] = value[
                     d * rows : (d + 1) * rows, t * chans : (t + 1) * chans
                 ]
         out0[zz] = term[1 - c, zz].astype(BF16)
@@ -215,11 +219,13 @@
     def to_near(k):
         zz = order[k]
         copies0[k].wait_recv()
-        out1[zz, 0] = (term[c, zz, 0, 1 - x] + in0[zz, 0, 1 - x].astype(F32)).astype(BF16)
-        by_x = send(out1.at[zz, 0], in1.at[zz, 0], s1.at[2 * k], r1.at[2 * k], x_peer)
-        out1[zz, 1] = (term[c, zz, 1, :, 1 - y] + in0[zz, 1, :, 1 - y].astype(F32)).astype(BF16)
-        by_y = send(out1.at[zz, 1], in1.at[zz, 1], s1.at[2 * k + 1], r1.at[2 * k + 1], y_peer)
-        copies1.append((by_x, by_y))
+        group1 = []
+        for i, (xx, yy, peer) in enumerate(near):
+            out1[zz, i] = (term[c, zz, xx, yy] + in0[zz, xx, yy].astype(F32)).astype(BF16)
+            group1.append(
+                send(out1.at[zz, i], in1.at[zz, i], s1.at[3 * k + i], r1.at[3 * k + i], peer)
+            )
+        copies1.append(group1)
 
     for k in range(depth):
         to_core(k)
@@ -228,49 +234,25 @@
     to_near(depth - 1)
     dwin[...] = dot(dpre_ref[...], kern[...], ((1,), (0,)))
 
-    def held(t, zz):
-        return (
-            term[c, zz, t, x, y]
-            + in0[zz, t, x, y].astype(F32)
-            + in1[zz, t, y if t == 0 else x].astype(F32)
-            + in2[zz, t].astype(F32)
-        )
-
-    copies2, copies3 = [], []
-
-    def to_z(k):
-        copies2[k][0].wait_recv()
-        copies2[k][1].wait_recv()
-        for t in range(2):
-            out3[k, t] = held(t, order[k]).astype(BF16)
+    def held(k):
+        zz = order[k]
+        for copy in copies1[k]:
+            copy.wait_recv()
+        value = term[c, zz, x, y] + in0[zz, x, y].astype(F32)
+        for i in range(3):
+            value = value + in1[zz, i].astype(F32)
+        return value
+
+    copies3 = []
+    for k in range(depth - 1):
+        out3[k] = held(k).astype(BF16)
         copies3.append(
             send(out3.at[k], in3.at[k], s3.at[k], r3.at[k], (me + 8 * (k + 1)) % n)
         )
-
-    for k, zz in enumerate(order):
-        copies1[k][0].wait_recv()
-        copies1[k][1].wait_recv()
-        out2[zz, 0] = (
-            term[c, zz, 0, x, 1 - y]
-            + in0[zz, 0, x, 1 - y].astype(F32)
-            + in1[zz, 0, 1 - y].astype(F32)
-        ).astype(BF16)
-        by_y = send(out2.at[zz, 0], in2.at[zz, 0], s2.at[2 * k], r2.at[2 * k], y_peer)
-        out2[zz, 1] = (
-            term[c, zz, 1, 1 - x, y]
-            + in0[zz, 1, 1 - x, y].astype(F32)
-            + in1[zz, 1, 1 - x].astype(F32)
-        ).astype(BF16)
-        by_x = send(out2.at[zz, 1], in2.at[zz, 1], s2.at[2 * k + 1], r2.at[2 * k + 1], x_peer)
-        copies2.append((by_y, by_x))
-        if k:
-            to_z(k - 1)
-    copies2[-1][0].wait_recv()
-    copies2[-1][1].wait_recv()
-    own = [held(t, z) for t in range(2)]
+    own = held(depth - 1)
     for k in range(depth - 1):
         copies3[k].wait_recv()
-        own = [own[t] + in3[k, t].astype(F32) for t in range(2)]
+        own = own + in3[k].astype(F32)
 
     squares = own[0] * own[0] + own[1] * own[1]
     fold = sum(squares[:, l * LANES : (l + 1) * LANES] for l in range(chans // LANES))
@@ -309,13 +291,9 @@
 
     upd, nm, nf, ns = adamw(grad[...], scale, master[...], first[...], second[...])
 
-    def piece(zz, yy, xx, half=None):
+    def piece(zz, yy, xx):
         start = (((zz * 2 + yy) * 2 + xx) * 2 + c) * width
-        size = width
-        if half is not None:
-            size = width // 2
-            start = start + half * size
-        return gathered.at[:, pl.ds(pl.multiple_of(start, LANES), size)]
+        return gathered.at[:, pl.ds(pl.multiple_of(start, LANES), width)]
 
     mine = piece(z, y, x)
     mine[...] = nm.astype(BF16)
@@ -324,15 +302,17 @@
     for j in range(1, depth):
         copy = send(mine, mine, zs_s.at[j - 1], zs_r.at[j - 1], (me + 8 * j) % n)
         arrive.append(copy)
-    fx, fy, cores = [], [], []
+    around, cores = [], []
     for j in range(depth):
         zz = (z + depth - j) % depth
         if j:
             arrive[j - 1].wait_recv()
         block = piece(zz, y, x)
-        fx.append(send(block, block, xs.at[j], xr.at[j], x_peer))
-        fy.append(send(block, block, ys.at[j], yr.at[j], y_peer))
-        cores.append(send(block, block, cs.at[4 * j], cr.at[4 * j], core_peer))
+        group1 = []
+        for i, (xx, yy, peer) in enumerate(near):
+            group1.append(send(block, block, near_s.at[3 * j + i], near_r.at[3 * j + i], peer))
+        around.append(group1)
+        cores.append(send(block, block, cs.at[4 * j + 3], cr.at[4 * j + 3], core_peer))
         if j == 0:
             update[...] = upd
             new_master[...] = nm
@@ -341,25 +321,12 @@
             for copy in norms:
                 copy.wait_send()
                 sent.remove(copy)
-    ex, ey = [], []
     for j in range(depth):
         zz = (z + depth - j) % depth
-        fy[j].wait_recv()
-        block = piece(zz, 1 - y, x)
-        half = piece(zz, 1 - y, x, 0)
-        ex.append(send(half, half, dxs.at[j], dxr.at[j], x_peer))
-        cores.append(send(block, block, cs.at[4 * j + 1], cr.at[4 * j + 1], core_peer))
-        fx[j].wait_recv()
-        block = piece(zz, y, 1 - x)
-        half = piece(zz, y, 1 - x, 1)
-        ey.append(send(half, half, dys.at[j], dyr.at[j], y_peer))
-        cores.append(send(block, block, cs.at[4 * j + 2], cr.at[4 * j + 2], core_peer))
-    for j in range(depth):
-        zz = (z + depth - j) % depth
-        ex[j].wait_recv()
-        ey[j].wait_recv()
-        block = piece(zz, 1 - y, 1 - x)
-        cores.append(send(block, block, cs.at[4 * j + 3], cr.at[4 * j + 3], core_peer))
+        for i in (1, 2, 0):
+            around[j][i].wait_recv()
+            block = piece(zz, near[i][1], near[i][0])
+            cores.append(send(block, block, cs.at[4 * j + i], cr.at[4 * j + i], core_peer))
     for copy in cores:
         copy.wait_recv()
     for copy in sent:
@@ -427,10 +394,8 @@
             pltpu.VMEM((2, depth, 2, 2, 2) + block, F32),
             pltpu.VMEM((depth, 2, 2, 2) + block, BF16),
             pltpu.VMEM((depth, 2, 2, 2) + block, BF16),
-            pltpu.VMEM((depth, 2, 2) + block, BF16),
-            pltpu.VMEM((depth, 2, 2) + block, BF16),
-            pltpu.VMEM((depth, 2) + block, BF16),
-            pltpu.VMEM((depth, 2) + block, BF16),
+            pltpu.VMEM((depth, 3, 2) + block, BF16),
+            pltpu.VMEM((depth, 3, 2) + block, BF16),
             pltpu.VMEM((depth, 2) + block, BF16),
             pltpu.VMEM((depth, 2) + block, BF16),
             pltpu.VMEM((1, LANES), F32),
@@ -438,12 +403,9 @@
             pltpu.VMEM(master.shape, F32),
             dma((9,)),
             dma((depth,)), dma((depth,)),
-            dma((2 * depth,)), dma((2 * depth,)),
-            dma((2 * depth,)), dma((2 * depth,)),
+            dma((3 * depth,)), dma((3 * depth,)),
             dma((depth,)), dma((depth,)), dma((n - 1,)), dma((n - 1,)),
-            dma((depth,)), dma((depth,)),
-            dma((depth,)), dma((depth,)), dma((depth,)), dma((depth,)),
-            dma((depth,)), dma((depth,)), dma((depth,)), dma((depth,)),
+            dma((depth,)), dma((depth,)), dma((3 * depth,)), dma((3 * depth,)),
             dma((4 * depth,)), dma((4 * depth,)),
         ],
         compiler_params=pltpu.CompilerParams(

time: 41.2 us -> 37.4 us (0.908)
  Pallas kernels: 40.4 us -> 36.6 us
    pallas_call x1, Pallas kernels: 39 us -> 35.3 us  [kernel_body(): pl.pallas_call(functools.partial(step_kernel, n, frames_out), out_shape=o...]
where the time goes in v5:
time: 37.4 us; the launch traced here: 37.3 us
  Pallas kernels  36.6 us (98%)
  between operations  0.64 us (2%)
    pallas_call x1, Pallas kernels, kernel_body(): pl.pallas_call(functools.partial(step_kernel, n, frames_out), out_shape=o...  35.3 us
    pallas_call x1, Pallas kernels, kernel_body(): pl.pallas_call(hand_over, out_shape=outs, in_specs=[vmem] * 6, out_specs=...  1.38 us

profile of v5, /device:TPU:0, one launch (start us, length us, event | category | flops | bytes accessed | tf_op | source)
XLA Modules:
  0.0 37.3 jit_solution(5374417591897697316)
XLA Ops:
  0.6 35.3 %conv_step.1 = (bf16[199,4,512]{2,1,0:T(4,128)(2,1)S(1)}, f32[2,8192]{1,0:T(2,128)S(1)}, f32[2,8192]{1,0:T(2,128)S(1)}, f32[2,8192]{1,0:T(2,128)S(1)}, f32[2,819...) custom-call(bf16[199,4,512]{2,1,0:T(4,128)(2,1)} %bitcast.4, bf16[2,262144]{1,0:T(2,128)(2,1)} %weights_hbm.1, ...), custom_call_target="tpu_custom_call" | custom-call | tf_op jit(solution)/shard_map/conv_step/pallas_call | solution.py:373
  35.9 1.4 %hand_over.1 = (bf16[199,4,512]{2,1,0:T(4,128)(2,1)}, f32[2,8192]{1,0:T(2,128)}, f32[2,8192]{1,0:T(2,128)}, f32[2,8192]{1,0:T(2,128)}, f32[2,8192]{1,0:T(2,128)}, /*index=5*/bf16[2,262144]{1,0:T(2,128)(2,1)}) custom-call(bf16[199,4,512]{2,1,0:T(4,128)(2,1)S(1)} %get-tuple-element.18.refs_0_, f32[2,8192]{1,0:T(2,128)S(1)} %get-tuple-element.19.refs_1_, ...), custom_call_target="tpu_custom_call" | custom-call | tf_op jit(solution)/shard_map/hand_over/pallas_call | solution.py:424

commit v6 on v5

--- a/solution.py
+++ b/solution.py
@@ -114,7 +114,7 @@
             )
         )
     ]
-    for copy in loads:
+    for copy in loads[:4]:
         copy.start()
 
     barrier = pltpu.get_barrier_semaphore()
@@ -130,6 +130,8 @@
     if pad_rows > live_rows:
         win[live_rows:pad_rows, :] = jnp.zeros((pad_rows - live_rows, 2 * chans), BF16)
     loads[1].wait()
+    for copy in loads[4:]:
+        copy.start()
     group = 64 if chans % 64 == 0 else 16
 
     @pl.loop(0, chans // group)
@@ -185,7 +187,11 @@
         tilt = jnp.mean(dn * nrm, axis=-1, keepdims=True)
         dpre_ref[part, :] = (dn - low - nrm * tilt).astype(BF16)
 
-    sent = []
+    def drain(ref, sem):
+        pltpu.make_async_copy(ref, ref, sem).wait()
+
+    def every(count):
+        return gathered.at[:, pl.ds(0, count * width)]
 
     def send(src, dst, ssem, rsem, peer):
         copy = pltpu.make_async_remote_copy(
@@ -193,12 +199,10 @@
             device_id=(peer,), device_id_type=MESH,
         )
         copy.start()
-        sent.append(copy)
         return copy
 
     order = [(z + j) % depth for j in range(1, depth)] + [z]
     copies0 = []
-    copies1 = []
 
     def to_core(k):
         zz = order[k]
@@ -219,13 +223,9 @@
     def to_near(k):
         zz = order[k]
         copies0[k].wait_recv()
-        group1 = []
         for i, (xx, yy, peer) in enumerate(near):
             out1[zz, i] = (term[c, zz, xx, yy] + in0[zz, xx, yy].astype(F32)).astype(BF16)
-            group1.append(
-                send(out1.at[zz, i], in1.at[zz, i], s1.at[3 * k + i], r1.at[3 * k + i], peer)
-            )
-        copies1.append(group1)
+            send(out1.at[zz, i], in1.at[zz, i], s1.at[k], r1.at[k], peer)
 
     for k in range(depth):
         to_core(k)
@@ -236,8 +236,7 @@
 
     def held(k):
         zz = order[k]
-        for copy in copies1[k]:
-            copy.wait_recv()
+        drain(in1.at[zz], r1.at[k])
         value = term[c, zz, x, y] + in0[zz, x, y].astype(F32)
         for i in range(3):
             value = value + in1[zz, i].astype(F32)
@@ -257,13 +256,8 @@
     squares = own[0] * own[0] + own[1] * own[1]
     fold = sum(squares[:, l * LANES : (l + 1) * LANES] for l in range(chans // LANES))
     sq_out[...] = jnp.sum(fold, axis=0, keepdims=True)
-    earlier = tuple(sent)
-    sent.clear()
-    norms = []
     for j in range(1, n):
-        norms.append(
-            send(sq_out, sq_in.at[pl.ds(j - 1, 1)], sq_s.at[j - 1], sq_r.at[j - 1], (me + j) % n)
-        )
+        send(sq_out, sq_in.at[pl.ds(j - 1, 1)], sq_s, sq_r, (me + j) % n)
     for r in range(rows):
         for t in range(2):
             grad[t : t + 1, r * chans : (r + 1) * chans] = own[t][r : r + 1, :]
@@ -282,10 +276,11 @@
         dinput[2 * frames_out : frames_in] = jnp.zeros(
             (frames_in - 2 * frames_out, clips, chans), BF16
         )
-    for copy in earlier:
+    for k, zz in enumerate(order):
+        drain(out1.at[zz], s1.at[k])
+    for copy in copies0 + copies3:
         copy.wait_send()
-    for copy in norms:
-        copy.wait_recv()
+    drain(sq_in, sq_r)
     total = jnp.sum(sq_in[...]) + jnp.sum(sq_out[...])
     scale = jnp.minimum(1.0, 1.0 / (jnp.sqrt(jnp.full((1, 1), total)) + 1e-06))
 
@@ -302,35 +297,36 @@
     for j in range(1, depth):
         copy = send(mine, mine, zs_s.at[j - 1], zs_r.at[j - 1], (me + 8 * j) % n)
         arrive.append(copy)
-    around, cores = [], []
+    around = []
     for j in range(depth):
         zz = (z + depth - j) % depth
         if j:
             arrive[j - 1].wait_recv()
         block = piece(zz, y, x)
-        group1 = []
-        for i, (xx, yy, peer) in enumerate(near):
-            group1.append(send(block, block, near_s.at[3 * j + i], near_r.at[3 * j + i], peer))
-        around.append(group1)
-        cores.append(send(block, block, cs.at[4 * j + 3], cr.at[4 * j + 3], core_peer))
+        around.append(
+            [
+                send(block, block, near_s, near_r.at[3 * j + i], peer)
+                for i, (xx, yy, peer) in enumerate(near)
+            ]
+        )
+        send(block, block, cs, cr, core_peer)
         if j == 0:
             update[...] = upd
             new_master[...] = nm
             new_first[...] = nf
             new_second[...] = ns
-            for copy in norms:
-                copy.wait_send()
-                sent.remove(copy)
+            drain(sq_in, sq_s)
     for j in range(depth):
         zz = (z + depth - j) % depth
         for i in (1, 2, 0):
             around[j][i].wait_recv()
             block = piece(zz, near[i][1], near[i][0])
-            cores.append(send(block, block, cs.at[4 * j + i], cr.at[4 * j + i], core_peer))
-    for copy in cores:
-        copy.wait_recv()
-    for copy in sent:
+            send(block, block, cs, cr, core_peer)
+    for copy in arrive:
         copy.wait_send()
+    drain(every(3 * depth), near_s)
+    drain(every(4 * depth), cs)
+    drain(every(4 * depth), cr)
 
 
 def hand_over(*refs):
@@ -403,10 +399,10 @@
             pltpu.VMEM(master.shape, F32),
             dma((9,)),
             dma((depth,)), dma((depth,)),
-            dma((3 * depth,)), dma((3 * depth,)),
-            dma((depth,)), dma((depth,)), dma((n - 1,)), dma((n - 1,)),
-            dma((depth,)), dma((depth,)), dma((3 * depth,)), dma((3 * depth,)),
-            dma((4 * depth,)), dma((4 * depth,)),
+            dma((depth,)), dma((depth,)),
+            dma((depth,)), dma((depth,)), dma, dma,
+            dma((depth,)), dma((depth,)), dma, dma((3 * depth,)),
+            dma, dma,
         ],
         compiler_params=pltpu.CompilerParams(
             collective_id=0, has_side_effects=True, vmem_limit_bytes=40 * 1024 * 1024

time: 37.4 us -> 36.4 us (0.973)
  Pallas kernels: 36.6 us -> 35.6 us
    pallas_call x1, Pallas kernels: 35.3 us -> 34.2 us  [kernel_body(): pl.pallas_call(functools.partial(step_kernel, n, frames_out), out_shape=o...]
where the time goes in v6:
time: 36.4 us; the launch traced here: 36.2 us
  Pallas kernels  35.6 us (98%)
  between operations  0.64 us (2%)
    pallas_call x1, Pallas kernels, kernel_body(): pl.pallas_call(functools.partial(step_kernel, n, frames_out), out_shape=o...  34.2 us
    pallas_call x1, Pallas kernels, kernel_body(): pl.pallas_call(hand_over, out_shape=outs, in_specs=[vmem] * 6, out_specs=...  1.38 us

profile of v6, /device:TPU:0, one launch (start us, length us, event | category | flops | bytes accessed | tf_op | source)
XLA Modules:
  0.0 36.2 jit_solution(13249079870455230182)
XLA Ops:
  0.6 34.2 %conv_step.1 = (bf16[199,4,512]{2,1,0:T(4,128)(2,1)S(1)}, f32[2,8192]{1,0:T(2,128)S(1)}, f32[2,8192]{1,0:T(2,128)S(1)}, f32[2,8192]{1,0:T(2,128)S(1)}, f32[2,819...) custom-call(bf16[199,4,512]{2,1,0:T(4,128)(2,1)} %bitcast.4, bf16[2,262144]{1,0:T(2,128)(2,1)} %weights_hbm.1, ...), custom_call_target="tpu_custom_call" | custom-call | tf_op jit(solution)/shard_map/conv_step/pallas_call | solution.py:369
  34.9 1.4 %hand_over.1 = (bf16[199,4,512]{2,1,0:T(4,128)(2,1)}, f32[2,8192]{1,0:T(2,128)}, f32[2,8192]{1,0:T(2,128)}, f32[2,8192]{1,0:T(2,128)}, f32[2,8192]{1,0:T(2,128)}, /*index=5*/bf16[2,262144]{1,0:T(2,128)(2,1)}) custom-call(bf16[199,4,512]{2,1,0:T(4,128)(2,1)S(1)} %get-tuple-element.18.refs_0_, f32[2,8192]{1,0:T(2,128)S(1)} %get-tuple-element.19.refs_1_, ...), custom_call_target="tpu_custom_call" | custom-call | tf_op jit(solution)/shard_map/hand_over/pallas_call | solution.py:420

commit v7 on v6

--- a/solution.py
+++ b/solution.py
@@ -149,9 +149,11 @@
     bias = bias_ref[...]
     step = 80 if pad_rows % 80 == 0 else 16
 
+    short = step // 2
+
     def forward(i, fold):
-        base = pl.multiple_of(i * step, 16)
-        part = pl.ds(base, step)
+        base = pl.multiple_of(i * short, 8)
+        part = pl.ds(base, short)
         pre = pre_ref[part, :]
         center = pre - jnp.mean(pre, axis=-1, keepdims=True)
         spread = jnp.mean(center * center, axis=-1, keepdims=True)
@@ -160,13 +162,13 @@
         h = nrm * gain + bias
         cdf = 0.5 + 0.5 * lax.erf(h * (0.5**0.5))
         pdf = jnp.exp(-0.5 * h * h) * 0.3989422804014327
-        live = lax.broadcasted_iota(jnp.int32, (step, 1), 0) < live_rows - base
+        live = lax.broadcasted_iota(jnp.int32, (short, 1), 0) < live_rows - base
         act = jnp.where(live, h * cdf, 0.0)
         slope[part, :] = (cdf + h * pdf) * (gain * jnp.where(live, inv, 0.0))
         pre_ref[part, :] = nrm
-        return fold + jnp.sum(act.reshape(step // 8, 8, chans), axis=0)
-
-    fold = lax.fori_loop(0, pad_rows // step, forward, jnp.zeros((8, chans), F32))
+        return fold + jnp.sum(act.reshape(short // 8, 8, chans), axis=0)
+
+    fold = lax.fori_loop(0, pad_rows // short, forward, jnp.zeros((8, chans), F32))
     pooled = fold
     for k in range(1, 8 // clips):
         pooled = pooled + pltpu.roll(fold, k * clips, 0)

time: 36.4 us -> 37.2 us (1.022)
  Pallas kernels: 35.6 us -> 36.4 us
    pallas_call x1, Pallas kernels: 34.2 us -> 35 us  [kernel_body(): pl.pallas_call(functools.partial(step_kernel, n, frames_out), out_shape=o...]
where the time goes in v7:
time: 37.2 us; the launch traced here: 37.1 us
  Pallas kernels  36.4 us (98%)
  between operations  0.64 us (2%)
    pallas_call x1, Pallas kernels, kernel_body(): pl.pallas_call(functools.partial(step_kernel, n, frames_out), out_shape=o...  35 us
    pallas_call x1, Pallas kernels, kernel_body(): pl.pallas_call(hand_over, out_shape=outs, in_specs=[vmem] * 6, out_specs=...  1.38 us

profile of v7, /device:TPU:0, one launch (start us, length us, event | category | flops | bytes accessed | tf_op | source)
XLA Modules:
  0.0 37.1 jit_solution(15576478265245929977)
XLA Ops:
  0.6 35.0 %conv_step.1 = (bf16[199,4,512]{2,1,0:T(4,128)(2,1)S(1)}, f32[2,8192]{1,0:T(2,128)S(1)}, f32[2,8192]{1,0:T(2,128)S(1)}, f32[2,8192]{1,0:T(2,128)S(1)}, f32[2,819...) custom-call(bf16[199,4,512]{2,1,0:T(4,128)(2,1)} %bitcast.4, bf16[2,262144]{1,0:T(2,128)(2,1)} %weights_hbm.1, ...), custom_call_target="tpu_custom_call" | custom-call | tf_op jit(solution)/shard_map/conv_step/pallas_call | solution.py:371
  35.7 1.4 %hand_over.1 = (bf16[199,4,512]{2,1,0:T(4,128)(2,1)}, f32[2,8192]{1,0:T(2,128)}, f32[2,8192]{1,0:T(2,128)}, f32[2,8192]{1,0:T(2,128)}, f32[2,8192]{1,0:T(2,128)}, /*index=5*/bf16[2,262144]{1,0:T(2,128)(2,1)}) custom-call(bf16[199,4,512]{2,1,0:T(4,128)(2,1)S(1)} %get-tuple-element.18.refs_0_, f32[2,8192]{1,0:T(2,128)S(1)} %get-tuple-element.19.refs_1_, ...), custom_call_target="tpu_custom_call" | custom-call | tf_op jit(solution)/shard_map/hand_over/pallas_call | solution.py:422
